TPU v7x, 128 devices: a whole 4x4x4 slice. The times are simulated.
128 devices in a mesh: seq: 32 (over x, z, core), head: 4 (over y).
Axes of the slice: x: 4, y: 4, z: 4, core: 2. Of those that a mesh axis runs over, the one named last changes fastest.
Arguments:
- queries: bfloat16 [16384, 5120], P('seq', 'head'), may hold values from -13 to 13, as said below
- keys: bfloat16 [16384, 1024], P('seq', 'head'), may hold values from -13 to 13, as said below
- values: bfloat16 [16384, 1024], P('seq', 'head'), may hold values from -6 to 6
- out_weight: bfloat16 [5120, 2560], P('head', 'seq'), may hold values from -0.078125 to 0.078125
- d_proj: bfloat16 [16384, 2560], P('seq', 'head'), may hold values from -6 to 6
- block_section: int32 [128], replicated, may hold values from 0 to 15, as said below
- section_parent: int32 [16], replicated, may hold values from -1 to 14, as said below
- xref_owner: int32 [1536, 1], P('seq'), may hold values from 0 to 31; in each aligned block of 48 rows (0 to 47, 48 to 95, ...) at most 2 rows name the same one
- xref_block: int32 [128, 12], P('seq'), may hold values from 0 to 3
- xref_valid: int32 [128, 12], P('seq'), may hold values 0 or 1
Outputs:
- projected: bfloat16 [16384, 2560], P('seq', 'head')
- d_queries: bfloat16 [16384, 5120], P('seq', 'head')
- d_keys: bfloat16 [16384, 1024], P('seq', 'head')
- d_values: bfloat16 [16384, 1024], P('seq', 'head')
Inputs may be any that keep to these rules, and one draw needn't show every extreme that they name: `queries`: entries of order one; a few rows of larger norm. `keys`: entries of order one; a few rows of larger norm. section_parent[s] is an earlier section for s > 0, and section_parent[0] = -1. `block_section`: sections are runs of consecutive blocks, 2 to 14 blocks each, some section exactly 14; no section begins at a block whose index is a positive multiple of 4. `xref_owner`: among the 48 rows of one device, no owner is named more than 2 times; some owner exactly 2 times.
All inputs are finite; a program needn't handle non-finite values. No bound on the sum of `xref_valid` on one device may be relied on, other than what follows from the above.
Results may differ from a plain program's by a relative error of at most 0.015.
The roundings to bfloat16 on the way count: a program that leaves them out, or rounds other values in their place, can miss the bound.
Values may be sent and summed in bfloat16 or wider, within the bound.
A program may use at most 192 MiB of HBM per device.

v0:
```python
import jax
import jax.numpy as jnp
from jax import lax
from jax.sharding import PartitionSpec as P

HEAD_DIMENSION = 128
BLK = 128
LOOK = 4
ANC = 2
XREF = 12


neg_large = -1e30


def passed_along(block, axis, distance):
    devices = range(lax.axis_size(axis))
    route = [(i - distance, i) for i in devices if i - distance in devices]
    return lax.ppermute(block, axis, route)


def query_layout(block, kv_heads):
    row_count = block.shape[0]
    group_size = block.shape[1] // (HEAD_DIMENSION * kv_heads)
    return block.reshape(row_count, kv_heads, group_size, HEAD_DIMENSION)


def key_layout(key_set, kv_heads):
    num_blocks, row_count, key_value_width = key_set.shape
    return key_set.reshape(num_blocks * row_count, kv_heads, HEAD_DIMENSION)


def softmax_weights(scores, allowed):
    masked = jnp.where(allowed, scores, neg_large)
    row_max = jnp.max(masked, axis=-1, keepdims=True)
    exponent = jnp.where(allowed, jnp.exp(masked - row_max), 0.0)
    return exponent / jnp.sum(exponent, axis=-1, keepdims=True)


def product(form, left, right):
    return jnp.einsum(form, left, right, preferred_element_type=jnp.float32)


def forward_block(query_block, key_set, value_set, allowed):
    kv_heads = key_set.shape[2] // HEAD_DIMENSION
    scaling = HEAD_DIMENSION ** (-0.5)
    query_heads = query_layout(query_block, kv_heads)
    key_heads = key_layout(key_set, kv_heads)
    value_heads = key_layout(value_set, kv_heads)
    scores = product("qcgd,kcd->cqgk", query_heads, key_heads) * scaling
    weights = softmax_weights(scores, allowed[None, :, None, :])
    output = product("cqgk,kcd->qcgd", weights.astype(jnp.bfloat16), value_heads)
    return output.reshape(query_block.shape[0], -1).astype(jnp.bfloat16)


def backward_block(query_block, key_set, value_set, allowed, attn, d_attn):
    kv_heads = key_set.shape[2] // HEAD_DIMENSION
    scaling = HEAD_DIMENSION ** (-0.5)
    num_blocks = key_set.shape[0]
    row_count = query_block.shape[0]
    query_heads = query_layout(query_block, kv_heads)
    key_heads = key_layout(key_set, kv_heads)
    value_heads = key_layout(value_set, kv_heads)
    scores = product("qcgd,kcd->cqgk", query_heads, key_heads) * scaling
    weights = softmax_weights(scores, allowed[None, :, None, :])
    light = weights.astype(jnp.bfloat16)
    grad_heads = query_layout(d_attn, kv_heads)
    attn_heads = query_layout(attn, kv_heads)
    delta = jnp.einsum(
        "qcgd,qcgd->cqg", grad_heads.astype(jnp.float32), attn_heads.astype(jnp.float32)
    )[..., None]
    d_weights = product("qcgd,kcd->cqgk", grad_heads, value_heads)
    d_scores = (weights * (d_weights - delta) * scaling).astype(jnp.bfloat16)
    grad_query = product("cqgk,kcd->qcgd", d_scores, key_heads)
    key_terms = product("cqgk,qcgd->kcd", d_scores, query_heads)
    value_terms = product("cqgk,qcgd->kcd", light, grad_heads)
    return (
        grad_query.reshape(row_count, -1).astype(jnp.bfloat16),
        key_terms.reshape(num_blocks, -1),
        value_terms.reshape(num_blocks, -1),
    )


def run_forward(operands):
    return forward_block(operands[0], operands[1], operands[2], operands[3])


def run_backward(operands):
    return backward_block(
        operands[0], operands[1], operands[2], operands[3], operands[4], operands[5]
    )


def on_device(
    queries,
    keys,
    values,
    out_weight,
    d_proj,
    block_section,
    section_parent,
    xref_owner,
    xref_block,
    xref_valid,
):
    seq_count = lax.axis_size("seq")
    seq_rank = lax.axis_index("seq")
    tok_local = queries.shape[0]
    blk_count = tok_local // BLK
    key_value_width = keys.shape[1]
    blk_width = BLK * key_value_width
    sections = section_parent.shape[0]
    behind = LOOK - 1
    key_count = LOOK + ANC + XREF
    first_blk = seq_rank * blk_count
    key_flat = keys.reshape(blk_count, blk_width)
    value_flat = values.reshape(blk_count, blk_width)
    section_ids = jnp.arange(sections, dtype=jnp.int32)
    my_sec = lax.dynamic_slice_in_dim(block_section, first_blk, blk_count)
    counts = jnp.sum((block_section[:, None] == section_ids[None, :]).astype(jnp.float32), axis=0)
    root_counts = jnp.sqrt(counts)
    mine = (section_ids[:, None] == my_sec[None, :]).astype(jnp.float32)
    chain = [my_sec]
    prior = chain[-1]
    chain.append(
        jnp.where(
            prior >= 0,
            jnp.sum(
                jnp.where(prior[:, None] == section_ids[None, :], section_parent[None, :], 0),
                axis=1,
            ),
            -1,
        )
    )
    ancestors = jnp.stack(chain, axis=1).reshape(-1)
    chosen_up = ancestors[:, None] == section_ids[None, :]
    prev_keys, prev_values = passed_along(
        (keys[tok_local - behind * BLK :], values[tok_local - behind * BLK :]), "seq", 1
    )
    extended_keys = jnp.concatenate([prev_keys, keys], axis=0).reshape(
        blk_count + behind, BLK, key_value_width
    )
    extended_values = jnp.concatenate([prev_values, values], axis=0).reshape(
        blk_count + behind, BLK, key_value_width
    )
    mine_light = mine.astype(jnp.bfloat16)
    part_keys = (
        jnp.dot(mine_light, key_flat, preferred_element_type=jnp.float32) / root_counts[:, None]
    )
    part_values = (
        jnp.dot(mine_light, value_flat, preferred_element_type=jnp.float32) / root_counts[:, None]
    )
    total_keys, total_values = (
        lax.psum(part_keys.astype(jnp.bfloat16), "seq").astype(jnp.float32),
        lax.psum(part_values.astype(jnp.bfloat16), "seq").astype(jnp.float32),
    )
    summary_keys = total_keys.astype(jnp.bfloat16)
    summary_values = total_values.astype(jnp.bfloat16)
    chosen_light = chosen_up.astype(jnp.bfloat16)
    up_keys = (
        jnp.dot(chosen_light, summary_keys, preferred_element_type=jnp.float32)
        .astype(jnp.bfloat16)
        .reshape(blk_count, ANC, BLK, key_value_width)
    )
    up_values = (
        jnp.dot(chosen_light, summary_values, preferred_element_type=jnp.float32)
        .astype(jnp.bfloat16)
        .reshape(blk_count, ANC, BLK, key_value_width)
    )
    owners = xref_owner.reshape(-1)
    wanted = xref_block.reshape(-1)
    slot_total = owners.shape[0]
    slot_cap = max(2, slot_total // seq_count)
    slot_order = jnp.arange(slot_total)
    slot_rank = jnp.sum(
        (owners[:, None] == owners[None, :]) & (slot_order[:, None] > slot_order[None, :]), axis=1
    )
    placed = (owners * slot_cap + slot_rank)[:, None] == jnp.arange(seq_count * slot_cap)[None, :]
    placed_light = placed.astype(jnp.bfloat16)
    request = jnp.sum(jnp.where(placed, wanted[:, None] + 1, 0), axis=0).reshape(
        seq_count, slot_cap
    )
    asked_for = lax.all_to_all(request, "seq", split_axis=0, concat_axis=0, tiled=True).reshape(-1)
    served = ((asked_for - 1)[:, None] == jnp.arange(blk_count)[None, :]).astype(jnp.bfloat16)
    out_keys = (
        jnp.dot(served, key_flat, preferred_element_type=jnp.float32)
        .astype(jnp.bfloat16)
        .reshape(seq_count, slot_cap, blk_width)
    )
    out_values = (
        jnp.dot(served, value_flat, preferred_element_type=jnp.float32)
        .astype(jnp.bfloat16)
        .reshape(seq_count, slot_cap, blk_width)
    )
    got_keys, got_values = (
        lax.all_to_all(out_keys, "seq", split_axis=0, concat_axis=0, tiled=True),
        lax.all_to_all(out_values, "seq", split_axis=0, concat_axis=0, tiled=True),
    )
    ref_keys = jnp.dot(
        placed_light,
        got_keys.reshape(seq_count * slot_cap, blk_width),
        preferred_element_type=jnp.float32,
    )
    ref_values = jnp.dot(
        placed_light,
        got_values.reshape(seq_count * slot_cap, blk_width),
        preferred_element_type=jnp.float32,
    )
    ref_keys = ref_keys.astype(jnp.bfloat16).reshape(blk_count, XREF, BLK, key_value_width)
    ref_values = ref_values.astype(jnp.bfloat16).reshape(blk_count, XREF, BLK, key_value_width)
    window_keys = jnp.stack(
        [extended_keys[offset : offset + blk_count] for offset in range(LOOK)], axis=1
    )
    window_values = jnp.stack(
        [extended_values[offset : offset + blk_count] for offset in range(LOOK)], axis=1
    )
    key_sets = jnp.concatenate([window_keys, up_keys, ref_keys], axis=1)
    value_sets = jnp.concatenate([window_values, up_values, ref_values], axis=1)
    positions = jnp.arange(BLK)
    causal = positions[None, :] <= positions[:, None]
    is_last = jnp.arange(LOOK) == LOOK - 1
    padded_sec = jnp.concatenate([jnp.full((behind,), -1, jnp.int32), block_section])
    extended_sec = lax.dynamic_slice_in_dim(padded_sec, first_blk, blk_count + behind)
    window_sec = jnp.stack(
        [extended_sec[offset : offset + blk_count] for offset in range(LOOK)], axis=1
    )
    own_ok = window_sec == my_sec[:, None]
    own_allowed = own_ok[:, None, :, None] & (
        jnp.logical_not(is_last)[None, None, :, None] | causal[None, :, None, :]
    )
    up_allowed = jnp.broadcast_to(
        (ancestors >= 0).reshape(blk_count, ANC)[:, None, :, None], (blk_count, BLK, ANC, BLK)
    )
    ref_allowed = jnp.broadcast_to((xref_valid > 0)[:, None, :, None], (blk_count, BLK, XREF, BLK))
    allowed = jnp.concatenate([own_allowed, up_allowed, ref_allowed], axis=2).reshape(
        blk_count, BLK, key_count * BLK
    )
    query_blocks = queries.reshape(blk_count, BLK, -1)
    attn_blocks = lax.map(run_forward, (query_blocks, key_sets, value_sets, allowed))
    attn = attn_blocks.reshape(tok_local, -1)
    d_full = lax.all_gather(d_proj, "head", axis=1, tiled=True)
    partials = jnp.dot(
        attn,
        lax.all_gather(out_weight, "seq", axis=1, tiled=True),
        preferred_element_type=jnp.float32,
    )
    d_attn = lax.dot_general(
        d_full,
        lax.all_gather(out_weight, "seq", axis=1, tiled=True),
        (((1,), (1,)), ((), ())),
        preferred_element_type=jnp.float32,
    ).astype(jnp.bfloat16)
    projected = lax.psum_scatter(
        partials.astype(jnp.bfloat16), "head", scatter_dimension=1, tiled=True
    )
    grad_queries, key_terms, value_terms = lax.map(
        run_backward,
        (
            query_blocks,
            key_sets,
            value_sets,
            allowed,
            attn_blocks,
            d_attn.reshape(blk_count, BLK, -1),
        ),
    )

    def spread(terms):
        extended = jnp.zeros((blk_count + behind, blk_width), jnp.float32)
        for offset in range(LOOK):
            extended = extended.at[offset : offset + blk_count].add(terms[:, offset])
        return extended

    extended_dk = spread(key_terms)
    extended_dv = spread(value_terms)
    next_dk, next_dv = (
        passed_along(extended_dk[:behind].astype(jnp.bfloat16), "seq", -1).astype(jnp.float32),
        passed_along(extended_dv[:behind].astype(jnp.bfloat16), "seq", -1).astype(jnp.float32),
    )
    own_dk = extended_dk[behind:] + jnp.pad(next_dk, ((blk_count - behind, 0), (0, 0)))
    own_dv = extended_dv[behind:] + jnp.pad(next_dv, ((blk_count - behind, 0), (0, 0)))
    chosen_float = chosen_up.T.astype(jnp.float32)
    section_dk = jnp.dot(
        chosen_float,
        key_terms[:, LOOK : LOOK + ANC].reshape(blk_count * ANC, blk_width),
        precision=lax.Precision.HIGHEST,
    )
    section_dv = jnp.dot(
        chosen_float,
        value_terms[:, LOOK : LOOK + ANC].reshape(blk_count * ANC, blk_width),
        precision=lax.Precision.HIGHEST,
    )
    summed_dk, summed_dv = (
        lax.psum(section_dk.astype(jnp.bfloat16), "seq").astype(jnp.float32),
        lax.psum(section_dv.astype(jnp.bfloat16), "seq").astype(jnp.float32),
    )
    spread_down = (mine / root_counts[:, None]).T
    up_dk = jnp.dot(spread_down, summed_dk, precision=lax.Precision.HIGHEST)
    up_dv = jnp.dot(spread_down, summed_dv, precision=lax.Precision.HIGHEST)
    slot_dk_light = (
        key_terms[:, LOOK + ANC :].reshape(blk_count * XREF, blk_width).astype(jnp.bfloat16)
    )
    slot_dv_light = (
        value_terms[:, LOOK + ANC :].reshape(blk_count * XREF, blk_width).astype(jnp.bfloat16)
    )
    placed_back = placed_light.T
    slot_dk = (
        jnp.dot(placed_back, slot_dk_light, preferred_element_type=jnp.float32)
        .astype(jnp.bfloat16)
        .reshape(seq_count, slot_cap, blk_width)
    )
    slot_dv = (
        jnp.dot(placed_back, slot_dv_light, preferred_element_type=jnp.float32)
        .astype(jnp.bfloat16)
        .reshape(seq_count, slot_cap, blk_width)
    )
    back_dk, back_dv = (
        lax.all_to_all(slot_dk, "seq", split_axis=0, concat_axis=0, tiled=True),
        lax.all_to_all(slot_dv, "seq", split_axis=0, concat_axis=0, tiled=True),
    )
    served_back = served.T
    ref_dk = jnp.dot(
        served_back,
        back_dk.reshape(seq_count * slot_cap, blk_width),
        preferred_element_type=jnp.float32,
    )
    ref_dv = jnp.dot(
        served_back,
        back_dv.reshape(seq_count * slot_cap, blk_width),
        preferred_element_type=jnp.float32,
    )
    d_keys = (own_dk + up_dk + ref_dk).astype(jnp.bfloat16).reshape(tok_local, key_value_width)
    d_values = (own_dv + up_dv + ref_dv).astype(jnp.bfloat16).reshape(tok_local, key_value_width)
    return (projected, grad_queries.reshape(tok_local, -1), d_keys, d_values)


def solution(mesh):
    placed = (
        P("seq", "head"),
        P("seq", "head"),
        P("seq", "head"),
        P("head", "seq"),
        P("seq", "head"),
        P(),
        P(),
        P("seq", None),
        P("seq", None),
        P("seq", None),
    )
    return jax.shard_map(
        on_device,
        mesh=mesh,
        in_specs=placed,
        out_specs=(P("seq", "head"), P("seq", "head"), P("seq", "head"), P("seq", "head")),
        check_vma=False,
    )
```

profile of v0, /device:TPU:1, one launch (start us, length us, event | category | flops | bytes accessed | tf_op | source)
XLA Modules:
  0.0 869.6 jit_solution(12914485448332251548)
XLA Ops:
  15.8 16.2 %all_to_all.29 = s32[32,1,2]{2,1,0:T(1,128)S(1)} all-to-all(s32[32,1,2]{2,1,0:T(1,128)S(1)} %bitcast.243), channel_id=1, replica_groups=mesh['seq'=32,'head'=4] {'seq'}, dimensions={0} | all-to-all | bytes 512 | tf_op jit(solution)/shard_map/all_to_all | solution.py:183
  35.5 7.7 reshape.489
  43.2 5.3 all-to-all-start.2
  48.5 3.5 collective-permute-start
  58.9 7.7 reshape.482
  66.6 37.1 %all-to-all-done.2 = bf16[32,2,32768]{2,1,0:T(2,128)(2,1)} async-done(((bf16[32,2,32768]{2,1,0:T(2,128)(2,1)}), bf16[32,2,32768]{2,1,0:T(2,128)(2,1)}, u32[]{:S(2)}, u32[]{:S(2)}) %all-to-all-start.2) | async-done | bytes 4194336 | tf_op jit(solution)/shard_map/all_to_all | solution.py:196
  103.7 7.6 all-to-all-start.1
  123.4 83.3 %all-reduce.12.cloned.1.call-done = (bf16[16,32768]{1,0:T(8,128)(2,1)}, bf16[16,32768]{1,0:T(8,128)(2,1)}) async-done(((bf16[16,32768]{1,0:T(8,128)(2,1)}, bf16[16,32768]{1,0:T(8,128)(2,1)}), (bf16[16,32768]{1,0:T(8,128)(2,1)}, bf16[16,32768]{1,0:T(8,128)(2,1)})) %all-reduce.12.cloned.1.call-update) | async-done | bytes 2097168 | tf_op jit(solution)/shard_map/psum | solution.py:155
  211.8 7.2 reshape.490
  223.0 7.2 reshape.483
  237.3 94.8 %while.32 = (s32[]{:T(128)}, bf16[4,128,1280]{1,2,0:T(8,128)(2,1)}, bf16[4,18,128,256]{3,2,1,0:T(8,128)(2,1)}, pred[4,128,2304]{2,1,0:T(8,128)(4,1)}, bf16[4,128...) while((s32[]{:T(128)}, bf16[4,128,1280]{1,2,0:T(8,128)(2,1)}, ...), condition=%wide.region_9.10_spmd, body=%wide.region_6.9_spmd.sunk | while | flops 1530759424 | bytes 38250596 | solution.py:239
  243.4 10.6 %fusion.131 = (f32[2,128,5]{1,2,0:T(8,128)S(1)}, f32[2,128,5,2304]{3,1,2,0:T(8,128)}) fusion(pred[128,2304]{1,0:T(8,128)(4,1)} %dynamic-slice_bitcast_fusion.5, bf16[128,2,5,128]{0,3,2,1:T(8,128)(2,1)} %bitcast.225, bf16[2304,2,128,1]{2,1,0,3:T(2,128)(2,1)S(1)} %bitcast.219), kind=kOutput, calls=%fused_computation.165.clone.1 | convolution fusion | flops 769722624 | bytes 13603840 | tf_op jit(solution)/shard_map/while/body/eval_jaxpr/sub | solution.py:36
  254.0 6.4 fusion.132
  267.0 10.6 %fusion.131 = (f32[2,128,5]{1,2,0:T(8,128)S(1)}, f32[2,128,5,2304]{3,1,2,0:T(8,128)}) fusion(pred[128,2304]{1,0:T(8,128)(4,1)} %dynamic-slice_bitcast_fusion.5, bf16[128,2,5,128]{0,3,2,1:T(8,128)(2,1)} %bitcast.225, bf16[2304,2,128,1]{2,1,0,3:T(2,128)(2,1)S(1)} %bitcast.219), kind=kOutput, calls=%fused_computation.165.clone.1 | convolution fusion | flops 769722624 | bytes 13603840 | tf_op jit(solution)/shard_map/while/body/eval_jaxpr/sub | solution.py:36
  277.6 6.4 fusion.132
  290.6 10.6 %fusion.131 = (f32[2,128,5]{1,2,0:T(8,128)S(1)}, f32[2,128,5,2304]{3,1,2,0:T(8,128)}) fusion(pred[128,2304]{1,0:T(8,128)(4,1)} %dynamic-slice_bitcast_fusion.5, bf16[128,2,5,128]{0,3,2,1:T(8,128)(2,1)} %bitcast.225, bf16[2304,2,128,1]{2,1,0,3:T(2,128)(2,1)S(1)} %bitcast.219), kind=kOutput, calls=%fused_computation.165.clone.1 | convolution fusion | flops 769722624 | bytes 13603840 | tf_op jit(solution)/shard_map/while/body/eval_jaxpr/sub | solution.py:36
  301.2 6.4 fusion.132
  314.3 10.6 %fusion.131 = (f32[2,128,5]{1,2,0:T(8,128)S(1)}, f32[2,128,5,2304]{3,1,2,0:T(8,128)}) fusion(pred[128,2304]{1,0:T(8,128)(4,1)} %dynamic-slice_bitcast_fusion.5, bf16[128,2,5,128]{0,3,2,1:T(8,128)(2,1)} %bitcast.225, bf16[2304,2,128,1]{2,1,0,3:T(2,128)(2,1)S(1)} %bitcast.219), kind=kOutput, calls=%fused_computation.165.clone.1 | convolution fusion | flops 769722624 | bytes 13603840 | tf_op jit(solution)/shard_map/while/body/eval_jaxpr/sub | solution.py:36
  324.9 6.4 fusion.132
  334.5 8.3 convolution_convert_fusion.12
  342.7 227.1 %while.33 = (s32[]{:T(128)}, bf16[4,128,1280]{2,1,0:T(8,128)(2,1)}, f32[4,18,32768]{2,1,0:T(8,128)}, f32[4,18,32768]{2,1,0:T(8,128)}, bf16[4,18,128,256]{3,2,1,0...) while((s32[]{:T(128)}, bf16[4,128,1280]{2,1,0:T(8,128)(2,1)}, ...), condition=%wide.region_14.15_spmd, body=%wide.region_11.14_spmd.sunk | while | flops 3811083264 | bytes 115664048 | solution.py:256
  353.2 8.2 fusion.144
  361.5 7.1 fusion.145
  368.5 5.9 multiply_convert_fusion.2
  380.8 4.9 copy.208
  385.7 3.6 broadcast_in_dim.167
  389.3 4.8 broadcast_in_dim.168
  394.9 4.9 constant_dynamic-update-slice_fusion.25
  409.8 8.2 fusion.144
  418.0 7.1 fusion.145
  425.1 5.9 multiply_convert_fusion.2
  437.4 4.9 copy.208
  442.3 3.6 broadcast_in_dim.167
  445.9 4.8 broadcast_in_dim.168
  451.4 4.9 constant_dynamic-update-slice_fusion.25
  466.4 8.2 fusion.144
  474.6 7.1 fusion.145
  481.7 5.9 multiply_convert_fusion.2
  493.9 4.9 copy.208
  498.9 3.6 broadcast_in_dim.167
  502.5 4.8 broadcast_in_dim.168
  508.0 5.1 constant_dynamic-update-slice_fusion.25
  523.1 8.2 fusion.144
  531.3 7.1 fusion.145
  538.4 5.9 multiply_convert_fusion.2
  550.7 4.9 copy.208
  555.6 3.6 broadcast_in_dim.167
  559.2 4.8 broadcast_in_dim.168
  564.8 4.9 constant_dynamic-update-slice_fusion.25
  572.5 7.2 slice.344
  579.7 14.2 %copy.139 = f32[4,18,32768]{2,0,1:T(4,128)} copy(f32[4,18,32768]{2,1,0:T(8,128)} %get-tuple-element.189) | data formatting | bytes 18874368 | tf_op jit(solution)/shard_map/while | solution.py:256
  596.6 7.4 slice.345
  603.9 14.5 %copy.135 = f32[4,18,32768]{2,0,1:T(4,128)} copy(f32[4,18,32768]{2,1,0:T(8,128)} %get-tuple-element.188) | data formatting | bytes 18874368 | tf_op jit(solution)/shard_map/while | solution.py:256
  630.9 5.3 scatter-add.26
  638.5 5.3 scatter-add.29
  651.0 7.7 reshape.506
  658.7 6.0 all-to-all-start.4
  666.9 6.9 convolution_convert_fusion.11
  684.7 7.7 reshape.499
  695.5 24.1 %all-to-all-done.4 = bf16[32,2,32768]{2,1,0:T(2,128)(2,1)} async-done(((bf16[32,2,32768]{2,1,0:T(2,128)(2,1)}), bf16[32,2,32768]{2,1,0:T(2,128)(2,1)}, u32[]{:S(2)}, u32[]{:S(2)}) %all-to-all-start.4) | async-done | bytes 4194336 | tf_op jit(solution)/shard_map/all_to_all | solution.py:319
  719.6 7.6 all-to-all-start.3
  733.1 99.5 %all-reduce.10.cloned.1.call-done = (bf16[16,32768]{1,0:T(8,128)(2,1)}, bf16[16,32768]{1,0:T(8,128)(2,1)}) async-done(((bf16[16,32768]{1,0:T(8,128)(2,1)}, bf16[16,32768]{1,0:T(8,128)(2,1)}), (bf16[16,32768]{1,0:T(8,128)(2,1)}, bf16[16,32768]{1,0:T(8,128)(2,1)})) %all-reduce.10.cloned.1.call-update) | async-done | bytes 2097168 | tf_op jit(solution)/shard_map/psum | solution.py:294
  836.5 7.3 reshape.507
  848.0 7.2 reshape.500
  (261 shorter events, 206.7 us)
Async XLA Ops:
  8.0 198.7 %all-reduce.12.cloned.1.call-start = ((), (), s32[]{:S(2)}) async-start(), calls=%async_computation.10 | async-start | bytes 4194304 | tf_op jit(solution)/shard_map/psum | solution.py:155
  9.6 45.9 %copy-start.13 = (s32[4]{0:T(128)}, s32[4]{0:T(128)S(1)}, u32[]{:S(2)}) copy-start(s32[4]{0:T(128)S(1)} %dynamic_slice.39) | copy-start | bytes 52
  9.6 3.7 copy-start.15
  13.3 2.0 copy-start.18
  13.3 2.1 copy-start.20
  14.7 319.8 %all-gather.5.cloned.1.call-start = ((), (), s32[]{:S(2)}) async-start(), calls=%async_computation.7 | async-start | bytes 3276800 | tf_op jit(solution)/shard_map/all_gather | solution.py:241
  15.6 214.6 %copy-start.11 = (s32[48]{0:T(128)}, s32[48]{0:T(128)S(1)}, u32[]{:S(2)}) copy-start(s32[48]{0:T(128)S(1)} %fusion.74) | copy-start | bytes 580
  32.2 23.5 %copy-start.7 = (s32[64]{0:T(128)}, s32[64]{0:T(128)S(1)}, u32[]{:S(2)}) copy-start(s32[64]{0:T(128)S(1)} %sub.31) | copy-start | bytes 772
  43.1 5.3 copy-start.5
  43.1 8.9 %copy-start.4 = (bf16[512,256]{1,0:T(8,128)(2,1)S(1)}, bf16[512,256]{1,0:T(8,128)(2,1)}, u32[]{:S(2)}) copy-start(bf16[512,256]{1,0:T(8,128)(2,1)} %param.31) | copy-start | bytes 786436
  43.1 11.7 %copy-start.19 = (s32[128]{0:T(128)S(1)}, s32[128]{0:T(128)}, u32[]{:S(2)}) copy-start(s32[128]{0:T(128)} %param.35) | copy-start | bytes 1540
  43.1 11.8 %copy-start.21 = (s32[16]{0:T(128)S(1)}, s32[16]{0:T(128)}, u32[]{:S(2)}) copy-start(s32[16]{0:T(128)} %param.36) | copy-start | bytes 196
  43.1 12.5 %copy-start.17 = (s32[4,12]{1,0:T(4,128)S(1)}, s32[4,12]{1,0:T(4,128)}, u32[]{:S(2)}) copy-start(s32[4,12]{1,0:T(4,128)} %param.39) | copy-start | bytes 580
  43.2 60.6 %all-to-all-start.2 = ((bf16[32,2,32768]{2,1,0:T(2,128)(2,1)}), bf16[32,2,32768]{2,1,0:T(2,128)(2,1)}, u32[]{:S(2)}, u32[]{:S(2)}) async-start(bf16[32,2,32768]{2,1,0:T(2,128)(2,1)} %reshape.489), calls=%async_computation.2 | async-start | bytes 8388608 | tf_op jit(solution)/shard_map/all_to_all | solution.py:196
  48.4 286.1 %all-gather.3.cloned.1.call-start = ((), (), s32[]{:S(2)}) async-start(), calls=%async_computation.6 | async-start | bytes 6758400 | tf_op jit(solution)/shard_map/all_gather | solution.py:244
  48.5 68.9 %collective-permute-start = (bf16[384,256]{1,0:T(8,128)(2,1)S(1)}, bf16[384,256]{1,0:T(8,128)(2,1)S(1)}, u32[]{:S(2)}, u32[]{:S(2)}) collective-permute-start(bf16[384,256]{1,0:T(8,128)(2,1)S(1)} %slice.240), channel_id=1, source_target_pairs={{0,4},{4,8},{8,12},{12,16},{16,20},{20,24},{24,28},{28,32},{32,36}... | collective-permute-start | bytes 589832 | tf_op jit(solution)/shard_map/ppermute | solution.py:19
  52.8 63.7 %collective-permute-start.1 = (bf16[384,256]{1,0:T(8,128)(2,1)}, bf16[384,256]{1,0:T(8,128)(2,1)}, u32[]{:S(2)}, u32[]{:S(2)}) collective-permute-start(bf16[384,256]{1,0:T(8,128)(2,1)} %slice.248), channel_id=1, source_target_pairs={{0,4},{4,8},{8,12},{12,16},{16,20},{20,24},{24,28},{28,32},{32,36}... | collective-permute-start | bytes 589832 | tf_op jit(solution)/shard_map/ppermute | solution.py:19
  103.7 119.2 %all-to-all-start.1 = ((bf16[32,2,32768]{2,1,0:T(2,128)(2,1)}), bf16[32,2,32768]{2,1,0:T(2,128)(2,1)}, u32[]{:S(2)}, u32[]{:S(2)}) async-start(bf16[32,2,32768]{2,1,0:T(2,128)(2,1)} %reshape.482), calls=%async_computation.1 | async-start | bytes 8388608 | tf_op jit(solution)/shard_map/all_to_all | solution.py:197
  111.3 3.7 copy-start.6
  112.4 96.0 %copy-start.9 = (s32[8]{0:T(128)}, s32[8]{0:T(128)S(1)}, u32[]{:S(2)}) copy-start(s32[8]{0:T(128)S(1)} %eq.119) | copy-start | bytes 100
  361.5 7.1 copy-start
  418.0 7.1 copy-start
  474.6 7.1 copy-start
  531.3 7.1 copy-start
  603.9 15.2 %copy-start.10 = (s32[8]{0:T(128)S(1)}, s32[8]{0:T(128)}, u32[]{:S(2)}) copy-start(s32[8]{0:T(128)} %copy-done.9) | copy-start | bytes 100
  626.7 21.0 %copy-start.12 = (s32[48]{0:T(128)S(1)}, s32[48]{0:T(128)}, u32[]{:S(2)}) copy-start(s32[48]{0:T(128)} %copy-done.11) | copy-start | bytes 580
  645.1 198.8 %collective-permute-start.3 = (bf16[3,32768]{1,0:T(4,128)(2,1)S(1)}, bf16[3,32768]{1,0:T(4,128)(2,1)}, u32[]{:S(2)}, u32[]{:S(2)}) collective-permute-start(bf16[3,32768]{1,0:T(4,128)(2,1)S(1)} %slice.346), channel_id=1, source_target_pairs={{4,0},{8,4},{12,8},{16,12},{20,16},{24,20},{28,24},{32,28},{36,32}... | collective-permute-start | bytes 589832 | tf_op jit(solution)/shard_map/ppermute | solution.py:19
  658.7 60.9 %all-to-all-start.4 = ((bf16[32,2,32768]{2,1,0:T(2,128)(2,1)}), bf16[32,2,32768]{2,1,0:T(2,128)(2,1)}, u32[]{:S(2)}, u32[]{:S(2)}) async-start(bf16[32,2,32768]{2,1,0:T(2,128)(2,1)} %reshape.506), calls=%async_computation.4 | async-start | bytes 8388608 | tf_op jit(solution)/shard_map/all_to_all | solution.py:319
  664.7 168.0 %all-reduce.10.cloned.1.call-start = ((), (), s32[]{:S(2)}) async-start(), calls=%async_computation.9 | async-start | bytes 4194304 | tf_op jit(solution)/shard_map/psum | solution.py:294
  666.6 192.8 %reduce-scatter.4.cloned.1.call-start = ((), (), s32[]{:S(2)}) async-start(), calls=%async_computation.8 | async-start | bytes 3276800
  684.7 7.8 copy-start.3
  692.4 1.4 copy-start.1
  695.5 137.2 %copy-start.14 = (s32[4]{0:T(128)S(1)}, s32[4]{0:T(128)}, u32[]{:S(2)}) copy-start(s32[4]{0:T(128)} %copy-done.13) | copy-start | bytes 52
  695.5 137.2 %copy-start.16 = (f32[16]{0:T(128)S(1)}, f32[16]{0:T(128)}, u32[]{:S(2)}) copy-start(f32[16]{0:T(128)} %copy-done.15) | copy-start | bytes 196
  719.6 128.4 %all-to-all-start.3 = ((bf16[32,2,32768]{2,1,0:T(2,128)(2,1)}), bf16[32,2,32768]{2,1,0:T(2,128)(2,1)}, u32[]{:S(2)}, u32[]{:S(2)}) async-start(bf16[32,2,32768]{2,1,0:T(2,128)(2,1)} %reshape.499), calls=%async_computation.3 | async-start | bytes 8388608 | tf_op jit(solution)/shard_map/all_to_all | solution.py:318
  730.9 124.4 %collective-permute-start.2 = (bf16[3,32768]{1,0:T(4,128)(2,1)}, bf16[3,32768]{1,0:T(4,128)(2,1)}, u32[]{:S(2)}, u32[]{:S(2)}) collective-permute-start(bf16[3,32768]{1,0:T(4,128)(2,1)} %slice.347), channel_id=1, source_target_pairs={{4,0},{8,4},{12,8},{16,12},{20,16},{24,20},{28,24},{32,28},{36,32}... | collective-permute-start | bytes 589832 | tf_op jit(solution)/shard_map/ppermute | solution.py:19
  836.5 7.4 copy-start.2
  836.5 7.3 copy-start.8
Sparse Core Ops, SparseCore 0:
  14.8 191.8 all-reduce.11
  668.9 163.7 all-reduce.9
Sparse Core Ops, SparseCore 1:
  16.8 38.1 all-gather.4
  57.2 117.0 all-gather.2
  692.5 34.7 reduce-scatter.3
where the time goes:
time: 880 us; the launch traced here: 870 us
  local copies, waits for them, and re-layouts  324 us (37%)
  waiting for transfers between devices  245 us (28%)
  matrix products  220 us (25%)
  starting transfers between devices  37.2 us (4%)
  between operations  16.7 us (2%)
  blocking collectives  16.2 us (2%)
  other arithmetic  9.23 us (1%)
    psum x1, waiting for transfers between devices, on_device(): lax.psum(section_dk.astype(jnp.bfloat16), 'seq').astype(jnp.float32)  99.5 us
    dot_general x20, matrix products, product(): return jnp.einsum(form, left, right, preferred_element_type=jnp.float32)  89.6 us
    psum x1, waiting for transfers between devices, on_device(): lax.psum(part_values.astype(jnp.bfloat16), 'seq').astype(jnp.float32)  83.3 us
    sub x8, matrix products, softmax_weights(): exponent = jnp.where(allowed, jnp.exp(masked - row_max), 0.0)  75.3 us
    dynamic_slice x32, local copies, waits for them, and re-layouts, on_device(): lax.map(run_forward, (query_blocks, key_sets, value_sets, allowed))  37.6 us
    all_to_all x1, waiting for transfers between devices, on_device(): lax.all_to_all(out_keys, 'seq', split_axis=0, concat_axis=0, tiled=True)  37.1 us
    broadcast_in_dim x8, local copies, waits for them, and re-layouts, on_device(): lax.map(run_backward, (query_blocks, key_sets, value_sets, allowed, attn_...  33.5 us
    transpose x8, local copies, waits for them, and re-layouts, product(): return jnp.einsum(form, left, right, preferred_element_type=jnp.float32)  32.3 us
  transfers between devices with their start and end apart: 13, of which 4 were waited for; matrix products, arithmetic and copies ran while one was open for 27% of the time, Pallas kernels for 0%

commit v1 on v0

v1 whole, which is shorter than its diff:
```python
import functools
import jax, jax.numpy as jnp
from jax import lax
from jax.experimental import pallas as pl
from jax.experimental.pallas import tpu as pltpu
from jax.sharding import PartitionSpec as P
F32, BF = jnp.float32, jnp.bfloat16
MESH = pl.DeviceIdType.MESH
RING = 4


HD = 128
BLK = 128
LOG2E = 1.4426950408889634


def attention_kernel(NBLK, NSEC, NQ, G, XR, meta, q_ref, k_hbm, v_hbm, do_ref, attn_ref, dq_ref, dk_ref, dv_ref,
                     kc, vc, ak, av, sbuf, qs, dos, dot_t, ot, mrun, lrun, slots, counts, first, length, sems):
    scaling = HD ** -0.5
    NT = (((1,), (1,)), ((), ()))
    TN = (((0,), (0,)), ((), ()))
    NN = (((1,), (0,)), ((), ()))

    def mm(a, b, dims):
        return lax.dot_general(a, b, dims, preferred_element_type=F32)

    load_k = pltpu.make_async_copy(k_hbm, kc.at[pl.ds(0, NBLK * BLK)], sems.at[0])
    load_v = pltpu.make_async_copy(v_hbm, vc.at[pl.ds(0, NBLK * BLK)], sems.at[1])
    load_k.start()
    load_v.start()

    @pl.loop(0, NSEC)
    def _(s):
        length[s] = 0
        first[s] = 0

    @pl.loop(0, NBLK)
    def _(c):
        s = meta[4, c]
        n = length[s]

        @pl.when(n == 0)
        def _():
            first[s] = c
        length[s] = n + 1

    @pl.loop(0, NQ)
    def _(b):
        g = meta[6, 0] + b
        mine = meta[4, g]
        slots[b, 0] = g
        slots[b, 1] = NBLK + mine
        n = jnp.int32(2)
        for w in (1, 2, 3):
            c = g - w
            cs = jnp.maximum(c, 0)
            slots[b, n] = cs
            n = n + jnp.where((c >= 0) & (meta[4, cs] == mine), 1, 0)
        up = meta[5, mine]
        slots[b, n] = NBLK + jnp.maximum(up, 0)
        n = n + jnp.where(up >= 0, 1, 0)
        row = lax.div(b, 4) * 8 + lax.rem(b, 4)
        for j in range(XR):
            t = meta[row, j]
            slots[b, n] = jnp.maximum(t, 0) + 256
            n = n + jnp.where(t >= 0, 1, 0)
        counts[b] = n

    @pl.loop(0, (NBLK + NSEC) // 4)
    def _(i):
        at = pl.ds(pl.multiple_of(i * 512, 512), 512)
        ak[at, :] = jnp.zeros((512, HD), F32)
        av[at, :] = jnp.zeros((512, HD), F32)

    load_k.wait()
    load_v.wait()

    def block(ref, i):
        return ref[pl.ds(pl.multiple_of(i * BLK, BLK), BLK), :]

    def root(s):
        return jnp.sqrt(jnp.full((8, HD), jnp.maximum(length[s], 1)).astype(F32))[:1]

    @pl.loop(0, NSEC)
    def _(s):
        for ref in (kc, vc):
            total = lax.fori_loop(first[s], first[s] + length[s],
                                  lambda c, t: t + block(ref, c).astype(F32), jnp.zeros((BLK, HD), F32))
            ref[pl.ds(pl.multiple_of((NBLK + s) * BLK, BLK), BLK), :] = (total / root(s)).astype(BF)

    W = G * BLK
    row_id = lax.broadcasted_iota(jnp.int32, (2 * BLK, BLK), 0)
    col_id = lax.broadcasted_iota(jnp.int32, (2 * BLK, BLK), 1)
    open_one = (row_id <= col_id) | (row_id >= BLK)
    open_all = jnp.concatenate([open_one] * G, axis=1)
    c2 = scaling * LOG2E

    def fold(op, s):
        return op(s.reshape(s.shape[0] // 8, 8, W), axis=0)

    @pl.loop(0, NQ)
    def _(b):
        base = pl.multiple_of(b * BLK, BLK)
        for g in range(G):
            part = slice(g * BLK, (g + 1) * BLK)
            qs[part, :] = q_ref[pl.ds(base, BLK), part]
            d = do_ref[pl.ds(base, BLK), part]
            dos[part, :] = d
            dot_t[:, part] = d.astype(F32).T.astype(BF)
        n = counts[b]
        pairs = lax.div(n, 2)
        odd = lax.rem(n, 2) == 1

        def idx(i):
            return slots[b, i] & 255

        def pair(ref, j):
            return jnp.concatenate([block(ref, idx(2 * j)), block(ref, idx(2 * j + 1))], axis=0)

        def at2(j):
            return pl.ds(pl.multiple_of(j * 2 * BLK, 2 * BLK), 2 * BLK)

        last = pl.ds(pl.multiple_of((n - 1) * BLK, BLK), BLK)

        s0 = jnp.where(open_all, mm(pair(kc, 0), qs[...], NT), -1e30)
        sbuf[at2(0), :] = s0

        def score(j, m):
            s = mm(pair(kc, j), qs[...], NT)
            sbuf[at2(j), :] = s
            return jnp.maximum(m, fold(jnp.max, s))
        mrun[...] = lax.fori_loop(1, pairs, score, fold(jnp.max, s0))

        @pl.when(odd)
        def _():
            s = mm(block(kc, idx(n - 1)), qs[...], NT)
            sbuf[last, :] = s
            mrun[...] = jnp.maximum(mrun[...], fold(jnp.max, s))
        top = jnp.max(mrun[...], axis=0, keepdims=True) * c2

        def weigh(rows, v):
            e = jnp.exp2(sbuf[rows, :] * c2 - top)
            sbuf[rows, :] = e
            return fold(jnp.sum, e), mm(v, e.astype(BF), TN)

        lrun[...], ot[...] = weigh(at2(0), pair(vc, 0))

        def forward(j, l):
            dl, o = weigh(at2(j), pair(vc, j))
            ot[...] += o
            return l + dl
        lrun[...] = lax.fori_loop(1, pairs, forward, lrun[...])

        @pl.when(odd)
        def _():
            dl, o = weigh(last, block(vc, idx(n - 1)))
            ot[...] += o
            lrun[...] += dl
        rl = 1.0 / jnp.sum(lrun[...], axis=0, keepdims=True)
        o_t = (ot[...] * rl).astype(BF).astype(F32)
        delta = jnp.sum(o_t * dot_t[...].astype(F32), axis=0, keepdims=True) * scaling
        for g in range(G):
            part = slice(g * BLK, (g + 1) * BLK)
            attn_ref[pl.ds(base, BLK), part] = o_t[:, part].T.astype(BF)

        def put(acc, i, term):
            slot = slots[b, i]
            where = pl.ds(pl.multiple_of((slot & 255) * BLK, BLK), BLK)
            term = jnp.where(slot >= 256, term.astype(BF).astype(F32), term)
            acc[where, :] += term

        def back(rows, k, v):
            p = sbuf[rows, :] * rl
            dp = mm(v, dot_t[...], NN)
            ds = (p * (dp * scaling - delta)).astype(BF)
            return mm(ds, qs[...], NN), mm(p.astype(BF), dos[...], NN), mm(k, ds, TN)

        ot[...] = jnp.zeros((HD, W), F32)

        def backward(j, carry):
            dk, dv, dq = back(at2(j), pair(kc, j), pair(vc, j))
            for h in range(2):
                put(ak, 2 * j + h, dk[h * BLK:(h + 1) * BLK])
                put(av, 2 * j + h, dv[h * BLK:(h + 1) * BLK])
            ot[...] += dq
            return carry
        lax.fori_loop(0, pairs, backward, 0)

        @pl.when(odd)
        def _():
            dk, dv, dq = back(last, block(kc, idx(n - 1)), block(vc, idx(n - 1)))
            put(ak, n - 1, dk)
            put(av, n - 1, dv)
            ot[...] += dq
        for g in range(G):
            part = slice(g * BLK, (g + 1) * BLK)
            dq_ref[pl.ds(base, BLK), part] = ot[:, part].T.astype(BF)

    @pl.loop(0, NBLK)
    def _(c):
        s = meta[4, c]
        share = 1.0 / root(s)
        at = pl.ds(pl.multiple_of(c * BLK, BLK), BLK)
        dk_ref[at, :] = (ak[at, :] + block(ak, NBLK + s) * share).astype(BF)
        dv_ref[at, :] = (av[at, :] + block(av, NBLK + s) * share).astype(BF)


def attention(meta, q, k, v, do, NSEC=16, XR=12):
    NBLK = k.shape[0] // BLK
    NQ = q.shape[0] // BLK
    G = q.shape[1] // HD
    W = G * BLK
    slots_most = 6 + XR
    vm = pl.BlockSpec(memory_space=pltpu.VMEM)
    return pl.pallas_call(
        functools.partial(attention_kernel, NBLK, NSEC, NQ, G, XR),
        out_shape=(jax.ShapeDtypeStruct(q.shape, BF), jax.ShapeDtypeStruct(q.shape, BF),
                   jax.ShapeDtypeStruct(k.shape, BF), jax.ShapeDtypeStruct(k.shape, BF)),
        in_specs=[pl.BlockSpec(memory_space=pltpu.SMEM), vm, pl.BlockSpec(memory_space=pl.ANY),
                  pl.BlockSpec(memory_space=pl.ANY), vm],
        out_specs=(vm, vm, vm, vm),
        scratch_shapes=[
            pltpu.VMEM(((NBLK + NSEC) * BLK, HD), BF),
            pltpu.VMEM(((NBLK + NSEC) * BLK, HD), BF),
            pltpu.VMEM(((NBLK + NSEC) * BLK, HD), F32),
            pltpu.VMEM(((NBLK + NSEC) * BLK, HD), F32),
            pltpu.VMEM((slots_most * BLK, W), F32),
            pltpu.VMEM((W, HD), BF),
            pltpu.VMEM((W, HD), BF),
            pltpu.VMEM((HD, W), BF),
            pltpu.VMEM((HD, W), F32),
            pltpu.VMEM((8, W), F32),
            pltpu.VMEM((8, W), F32),
            pltpu.SMEM((NQ, 24), jnp.int32),
            pltpu.SMEM((NQ,), jnp.int32),
            pltpu.SMEM((NSEC,), jnp.int32),
            pltpu.SMEM((NSEC,), jnp.int32),
            pltpu.SemaphoreType.DMA((2,)),
        ],
        compiler_params=pltpu.CompilerParams(vmem_limit_bytes=60 * 1024 * 1024),
        cost_estimate=pl.CostEstimate(flops=18_000_000_000, bytes_accessed=24_000_000, transcendentals=12_000_000),
    )(meta, q, k, v, do)


class Links:
    def __init__(self, send_sems, recv_sems):
        s = lax.axis_index("seq")
        self.y = lax.axis_index("head")
        self.x = s // 8
        self.z = (s // 2) % RING
        self.c = s % 2
        self.send_sems, self.recv_sems = send_sems, recv_sems
        self.used = 0
        self.sent = []

    def device(self, axis, step):
        x, z, y, c = self.x, self.z, self.y, self.c
        if axis == "x":
            x = (x + step) % RING
        elif axis == "z":
            z = (z + step) % RING
        elif axis == "y":
            y = (y + step) % RING
        else:
            c = 1 - c
        return ((x * RING + z) * 2 + c, y)

    def everyone(self):
        return [self.device(a, d) for a in "xzy" for d in (1, RING - 1)] + [self.device("c", 1)]

    def barrier(self):
        sem = pltpu.get_barrier_semaphore()
        for device in self.everyone():
            pl.semaphore_signal(sem, inc=1, device_id=device, device_id_type=MESH)
        pl.semaphore_wait(sem, 7)

    def number(self):
        self.used += 1
        return self.used - 1

    def send(self, number, src, dst, axis, step):
        copy = pltpu.make_async_remote_copy(
            src_ref=src, dst_ref=dst, send_sem=self.send_sems.at[number], recv_sem=self.recv_sems.at[number],
            device_id=self.device(axis, step), device_id_type=MESH)
        copy.start()
        self.sent.append(copy)

    def arrived(self, number, dst):
        pltpu.make_async_remote_copy(
            src_ref=dst, dst_ref=dst, send_sem=self.send_sems.at[number], recv_sem=self.recv_sems.at[number],
            device_id=self.device("c", 1), device_id_type=MESH).wait_recv()

    def finish(self):
        for copy in self.sent:
            copy.wait_send()


class Gather:
    def __init__(self, links, array, rows, pitch, offset, split, a, b):
        self.L, self.array, self.rows, self.pitch, self.offset, self.split = links, array, rows, pitch, offset, split
        self.a, self.b = a, b
        self.na = [links.number() for _ in range(4)]
        self.nb = [[links.number() for _ in range(4)] for _ in range(4)]

    def at(self, da, db, half=None):
        L = self.L
        move = {self.a: da, self.b: db}
        x, z = (L.x + move["x"]) % RING, (L.z + move["z"]) % RING
        start, count = self.offset, self.rows
        if half == 0:
            count = self.split
        elif half == 1:
            start, count = self.offset + self.split, self.rows - self.split
        return self.array.at[pl.ds(pl.multiple_of((x * RING + z) * self.pitch + start, 16), count), :]

    def put(self, number, axis, step, da, db, half=None):
        self.L.send(number, self.at(da, db, half), self.at(da, db, half), axis, step)

    def begin(self):
        self.put(self.na[0], self.a, 1, 0, 0)
        self.put(self.na[1], self.a, 3, 0, 0)

    def spread(self, i, da):
        self.put(self.nb[i][0], self.b, 1, da, 0)
        self.put(self.nb[i][1], self.b, 3, da, 0)

    def near(self):
        self.L.arrived(self.na[0], self.at(3, 0))
        self.put(self.na[2], self.a, 1, 3, 0, 0)
        self.L.arrived(self.na[1], self.at(1, 0))
        self.put(self.na[3], self.a, 3, 1, 0, 1)
        self.spread(0, 0)
        self.spread(1, 3)
        self.spread(2, 1)

    def far(self):
        self.L.arrived(self.na[2], self.at(2, 0, 0))
        self.L.arrived(self.na[3], self.at(2, 0, 1))
        self.spread(3, 2)

    def relay(self, i):
        da = (0, 3, 1, 2)[i]
        self.L.arrived(self.nb[i][0], self.at(da, 3))
        self.put(self.nb[i][2], self.b, 1, da, 3, 0)
        self.L.arrived(self.nb[i][1], self.at(da, 1))
        self.put(self.nb[i][3], self.b, 3, da, 1, 1)

    def end(self, i):
        da = (0, 3, 1, 2)[i]
        self.L.arrived(self.nb[i][2], self.at(da, 2, 0))
        self.L.arrived(self.nb[i][3], self.at(da, 2, 1))


def gather_kernel(q, k, v, wt, dp, meta, qh, kall, vall, wall, dattn, metas, wbuf, dbuf, abuf, send_sems, recv_sems, own_sems):
    L = Links(send_sems, recv_sems)
    chip = L.x * RING + L.z
    other = 1 - L.c
    T = k.shape[0]
    HD = kall.shape[1]
    W = qh.shape[1]
    C = wt.shape[0]
    D = dp.shape[1]
    L.barrier()

    pairs = []

    def split(src, width, dst, first, rows):
        at = dst.at[pl.ds(pl.multiple_of(first, 16), rows), :]
        pairs.append((L.number(), src, width, dst, at, rows))

    mine = chip * 2 * T + L.c * T
    split(wt, W, wbuf, chip * 2 * C + L.c * C, C)
    split(k, HD, kall, mine, T)
    split(v, HD, vall, mine, T)
    split(q, W, qh, L.c * T, T)
    own = []
    for i, (number, src, width, dst, at, rows) in enumerate(pairs):
        L.send(number, src.at[:, pl.ds(pl.multiple_of(other * width, 128), width)], at, "c", 1)
        copy = pltpu.make_async_copy(src.at[:, pl.ds(pl.multiple_of(L.c * width, 128), width)], at, own_sems.at[i])
        copy.start()
        own.append(copy)
    n_meta = L.number()
    mrow = metas.at[L.c]
    L.send(n_meta, meta, mrow, "c", 1)
    own_meta = pltpu.make_async_copy(meta, mrow, own_sems.at[4])
    own_meta.start()

    def piece(core, dy, half=None):
        ref = dbuf.at[core * RING + (L.y + dy) % RING]
        if half is None:
            return ref
        return ref.at[pl.ds(half * (T // 2), T // 2), :]

    ny = [L.number() for _ in range(4)]
    nc = [L.number() for _ in range(4)]
    L.send(ny[0], dp, piece(L.c, 0), "y", 1)
    L.send(ny[1], dp, piece(L.c, 0), "y", 3)
    L.send(nc[0], dp, piece(L.c, 0), "c", 1)
    own_d = pltpu.make_async_copy(dp, piece(L.c, 0), own_sems.at[5])
    own_d.start()

    sibling = [chip * 2 * C + other * C, chip * 2 * T + other * T, chip * 2 * T + other * T, other * T]

    def both(i):
        number, src, width, dst, at, rows = pairs[i]
        L.arrived(number, dst.at[pl.ds(pl.multiple_of(sibling[i], 16), rows), :])
        own[i].wait()

    first_w = (C // 2 + 15) // 16 * 16
    w0 = Gather(L, wbuf, C, 2 * C, 0, first_w, "x", "z")
    w1 = Gather(L, wbuf, C, 2 * C, C, first_w, "z", "x")
    gk = Gather(L, kall, 2 * T, 2 * T, 0, T, "x", "z")
    gv = Gather(L, vall, 2 * T, 2 * T, 0, T, "z", "x")
    both(0)
    w0.begin()
    w1.begin()
    both(1)
    gk.begin()
    both(2)
    gv.begin()
    w0.near()
    w1.near()
    w0.far()
    w1.far()
    L.arrived(ny[0], piece(L.c, 3))
    L.send(ny[2], piece(L.c, 3, 0), piece(L.c, 3, 0), "y", 1)
    L.arrived(ny[1], piece(L.c, 1))
    L.send(ny[3], piece(L.c, 1, 1), piece(L.c, 1, 1), "y", 3)
    L.send(nc[1], piece(L.c, 3), piece(L.c, 3), "c", 1)
    L.send(nc[2], piece(L.c, 1), piece(L.c, 1), "c", 1)
    gk.near()
    gv.near()
    for i in range(4):
        w0.relay(i)
        w1.relay(i)
    gk.far()
    gv.far()
    L.arrived(ny[2], piece(L.c, 2, 0))
    L.arrived(ny[3], piece(L.c, 2, 1))
    L.send(nc[3], piece(L.c, 2), piece(L.c, 2), "c", 1)
    for i in range(2):
        gk.relay(i)
        gv.relay(i)
    for i in range(4):
        w0.end(i)
        w1.end(i)
    own_d.wait()
    for i, dy in enumerate((0, 3, 1, 2)):
        L.arrived(nc[i], piece(other, dy))
    keep = pltpu.make_async_copy(wbuf, wall, own_sems.at[6])
    keep.start()

    step = 256

    def product(core, t):
        rows = pl.ds(pl.multiple_of(t * step, step), step)
        total = jnp.zeros((step, W), F32)
        for y in range(RING):
            total += jnp.dot(dbuf[core * RING + y, rows, :], wbuf[y * D:(y + 1) * D, :], preferred_element_type=F32)
        abuf[pl.ds(pl.multiple_of(core * T + t * step, step), step), :] = total.astype(BF)

    def products(core):
        @pl.loop(0, T // step)
        def _(t):
            product(core, t)

    products(0)
    for i in range(2, 4):
        gk.relay(i)
        gv.relay(i)
    products(1)
    save = pltpu.make_async_copy(abuf, dattn, own_sems.at[7])
    save.start()
    for i in range(4):
        gk.end(i)
        gv.end(i)
    both(3)
    L.arrived(n_meta, metas.at[other])
    own_meta.wait()
    keep.wait()
    save.wait()
    L.finish()


def gather(q, k, v, wt, dp, meta, seq):
    T = k.shape[0]
    HD = k.shape[1] // 2
    W = q.shape[1] // 2
    C = wt.shape[0]
    D = dp.shape[1]
    anywhere = pl.BlockSpec(memory_space=pl.ANY)
    sems = 128
    return pl.pallas_call(
        gather_kernel,
        out_shape=(
            jax.ShapeDtypeStruct((2 * T, W), BF),
            jax.ShapeDtypeStruct((seq * T, HD), BF),
            jax.ShapeDtypeStruct((seq * T, HD), BF),
            jax.ShapeDtypeStruct((seq * C, W), BF),
            jax.ShapeDtypeStruct((2 * T, W), BF),
            jax.ShapeDtypeStruct((2,) + meta.shape, jnp.int32),
        ),
        in_specs=[anywhere] * 6,
        out_specs=(anywhere,) * 6,
        scratch_shapes=[
            pltpu.VMEM((seq * C, W), BF),
            pltpu.VMEM((2 * RING, T, D), BF),
            pltpu.VMEM((2 * T, W), BF),
            pltpu.SemaphoreType.DMA((sems,)),
            pltpu.SemaphoreType.DMA((sems,)),
            pltpu.SemaphoreType.DMA((8,)),
        ],
        compiler_params=pltpu.CompilerParams(
            collective_id=0, has_side_effects=True, vmem_limit_bytes=40 * 1024 * 1024),
        cost_estimate=pl.CostEstimate(flops=3_400_000_000, bytes_accessed=40_000_000, transcendentals=0),
    )(q, k, v, wt, dp, meta)


class Scatter:
    def __init__(self, links, source, buf, far, near, far2, near2, final, a, b, load_sem):
        self.L, self.source, self.buf = links, source, buf
        self.farr, self.nearr, self.far2, self.near2, self.final = far, near, far2, near2, final
        self.a, self.b = a, b
        self.rows = final.shape[0]
        self.nb = [[links.number() for _ in range(4)] for _ in range(4)]
        self.na = [links.number() for _ in range(4)]
        self.load = pltpu.make_async_copy(source, buf, load_sem)
        self.load.start()

    def where(self, da, db, half=None):
        L = self.L
        move = {self.a: da, self.b: db}
        x, z = (L.x + move["x"]) % RING, (L.z + move["z"]) % RING
        start, count = 0, self.rows
        if half is not None:
            count = self.rows // 2
            start = half * count
        return pl.ds(pl.multiple_of((x * RING + z) * self.rows + start, 16), count)

    def half(self, h):
        return pl.ds(h * (self.rows // 2), self.rows // 2)

    def begin(self, i):
        da = (2, 3, 1, 0)[i]
        for h, step in ((0, 1), (1, 3)):
            self.L.send(self.nb[i][h], self.source.at[self.where(da, 2, h), :], self.farr.at[i, h], self.b, step)

    def loaded(self):
        self.load.wait()

    def pass_on(self, i):
        da = (2, 3, 1, 0)[i]
        for h, step in ((0, 1), (1, 3)):
            self.L.arrived(self.nb[i][h], self.farr.at[i, h])
            at = self.where(da, step, h)
            self.buf[at, :] = (self.buf[at, :].astype(F32) + self.farr[i, h].astype(F32)).astype(BF)
            self.L.send(self.nb[i][2 + h], self.buf.at[self.where(da, step), :], self.nearr.at[i, h], self.b, step)

    def total(self, i, da, h):
        at = self.where(da, 0, h)
        part = self.half(h)
        return (self.buf[at, :].astype(F32) + self.nearr[i, 0, part, :].astype(F32)
                + self.nearr[i, 1, part, :].astype(F32))

    def close(self, i):
        da = (2, 3, 1, 0)[i]
        for h in range(2):
            self.L.arrived(self.nb[i][2 + h], self.nearr.at[i, h])
        if i == 0:
            for h, step in ((0, 1), (1, 3)):
                at = self.where(da, 0, h)
                self.buf[at, :] = self.total(i, da, h).astype(BF)
                self.L.send(self.na[h], self.buf.at[at, :], self.far2.at[h], self.a, step)
        elif i < 3:
            take = 1 if da == 3 else 0
            self.L.arrived(self.na[take], self.far2.at[take])
            for h in range(2):
                value = self.total(i, da, h)
                if h == take:
                    value += self.far2[take].astype(F32)
                self.buf[self.where(da, 0, h), :] = value.astype(BF)
            self.L.send(self.na[2 + take], self.buf.at[self.where(da, 0), :], self.near2.at[take], self.a, da)

    def finish(self):
        for take in range(2):
            self.L.arrived(self.na[2 + take], self.near2.at[take])
        for h in range(2):
            part = self.half(h)
            self.final[part, :] = (self.total(3, 0, h) + self.near2[0, part, :].astype(F32)
                                   + self.near2[1, part, :].astype(F32)).astype(BF)


def scatter_kernel(dk, dv, attn, wall, dq, proj, dqo, dko, dvo,
                   bufk, bufv, farr, nearr, far2, near2, final, there, here, halves, wholes, result,
                   send_sems, recv_sems, own_sems):
    L = Links(send_sems, recv_sems)
    other = 1 - L.c
    T = proj.shape[0]
    D = proj.shape[1]
    W = dq.shape[1]
    HD = dk.shape[1]
    L.barrier()
    sk = Scatter(L, dk, bufk, farr.at[0], nearr.at[0], far2.at[0], near2.at[0], final.at[0], "x", "z", own_sems.at[0])
    sv = Scatter(L, dv, bufv, farr.at[1], nearr.at[1], far2.at[1], near2.at[1], final.at[1], "z", "x", own_sems.at[1])
    for i in range(4):
        sk.begin(i)
        sv.begin(i)

    def rows_of(core):
        return pl.ds(pl.multiple_of(core * T, 16), T)

    def heads(ref, core, width):
        return ref.at[:, pl.ds(pl.multiple_of(core * width, 128), width)]

    n_q = L.number()
    L.send(n_q, dq.at[rows_of(other), :], heads(dqo, L.c, W), "c", 1)
    own_q = pltpu.make_async_copy(dq.at[rows_of(L.c), :], heads(dqo, L.c, W), own_sems.at[2])
    own_q.start()

    n_there = [L.number() for _ in range(4)]
    ny = [L.number() for _ in range(4)]
    order = (2, 1, 3, 0)

    def product(core, dy):
        y = (L.y + dy) % RING
        w = wall[pl.ds(pl.multiple_of(y * D, 16), D), :]
        return lax.dot_general(attn[rows_of(core), :], w, (((1,), (1,)), ((), ())), preferred_element_type=F32)

    def away(i):
        here[i] = product(other, order[i]).astype(BF)
        L.send(n_there[i], here.at[i], there.at[i], "c", 1)

    def mine(i):
        value = product(L.c, order[i])
        L.arrived(n_there[i], there.at[i])
        return value + there[i].astype(F32)

    mid = T // 2
    away(0)
    sk.loaded()
    sv.loaded()
    sk.pass_on(0)
    sv.pass_on(0)
    away(1)
    sk.pass_on(1)
    sv.pass_on(1)
    away(2)
    away(3)
    sk.pass_on(2)
    sv.pass_on(2)
    result[0] = mine(0).astype(BF)
    L.send(ny[0], result.at[0, pl.ds(0, mid), :], halves.at[0], "y", 1)
    L.send(ny[1], result.at[0, pl.ds(mid, mid), :], halves.at[1], "y", 3)
    sk.pass_on(3)
    sv.pass_on(3)
    sk.close(0)
    sv.close(0)
    value = mine(1)
    L.arrived(ny[0], halves.at[0])
    result[1] = jnp.concatenate([value[:mid] + halves[0].astype(F32), value[mid:]], axis=0).astype(BF)
    L.send(ny[2], result.at[1], wholes.at[0], "y", 1)
    value = mine(2)
    L.arrived(ny[1], halves.at[1])
    result[2] = jnp.concatenate([value[:mid], value[mid:] + halves[1].astype(F32)], axis=0).astype(BF)
    L.send(ny[3], result.at[2], wholes.at[1], "y", 3)
    for i in (1, 2):
        sk.close(i)
        sv.close(i)
    value = mine(3)
    L.arrived(ny[2], wholes.at[0])
    L.arrived(ny[3], wholes.at[1])
    result[3] = (value + wholes[0].astype(F32) + wholes[1].astype(F32)).astype(BF)
    own_p = pltpu.make_async_copy(result.at[3], proj, own_sems.at[3])
    own_p.start()
    outs = []
    for j, (s, out) in enumerate(((sk, dko), (sv, dvo))):
        s.close(3)
        s.finish()
        n = L.number()
        L.send(n, final.at[j, rows_of(other), :], heads(out, L.c, HD), "c", 1)
        own = pltpu.make_async_copy(final.at[j, rows_of(L.c), :], heads(out, L.c, HD), own_sems.at[4 + j])
        own.start()
        outs.append((n, out, own))
    L.arrived(n_q, heads(dqo, other, W))
    own_q.wait()
    own_p.wait()
    for n, out, own in outs:
        L.arrived(n, heads(out, other, HD))
        own.wait()
    L.finish()


def scatter(dk, dv, attn, wall, dq, D):
    T = dq.shape[0] // 2
    W = dq.shape[1]
    HD = dk.shape[1]
    anywhere = pl.BlockSpec(memory_space=pl.ANY)
    vmem = pl.BlockSpec(memory_space=pltpu.VMEM)
    sems = 64
    return pl.pallas_call(
        scatter_kernel,
        out_shape=(
            jax.ShapeDtypeStruct((T, D), BF),
            jax.ShapeDtypeStruct((T, 2 * W), BF),
            jax.ShapeDtypeStruct((T, 2 * HD), BF),
            jax.ShapeDtypeStruct((T, 2 * HD), BF),
        ),
        in_specs=[anywhere, anywhere, vmem, vmem, anywhere],
        out_specs=(anywhere,) * 4,
        scratch_shapes=[
            pltpu.VMEM(dk.shape, BF),
            pltpu.VMEM(dk.shape, BF),
            pltpu.VMEM((2, 4, 2, T, HD), BF),
            pltpu.VMEM((2, 4, 2, 2 * T, HD), BF),
            pltpu.VMEM((2, 2, T, HD), BF),
            pltpu.VMEM((2, 2, 2 * T, HD), BF),
            pltpu.VMEM((2, 2 * T, HD), BF),
            pltpu.VMEM((4, T, D), BF),
            pltpu.VMEM((4, T, D), BF),
            pltpu.VMEM((2, T // 2, D), BF),
            pltpu.VMEM((2, T, D), BF),
            pltpu.VMEM((4, T, D), BF),
            pltpu.SemaphoreType.DMA((sems,)),
            pltpu.SemaphoreType.DMA((sems,)),
            pltpu.SemaphoreType.DMA((6,)),
        ],
        compiler_params=pltpu.CompilerParams(
            collective_id=1, has_side_effects=True, vmem_limit_bytes=56 * 1024 * 1024),
        cost_estimate=pl.CostEstimate(flops=3_400_000_000, bytes_accessed=40_000_000, transcendentals=0),
    )(dk, dv, attn, wall, dq)


def on_device(queries, keys, values, out_weight, d_proj, block_section, section_parent, xref_owner, xref_block, xref_valid):
    seq = lax.axis_size("seq")
    blocks, xrefs = xref_block.shape
    target = jnp.where(xref_valid > 0, xref_owner.reshape(blocks, xrefs) * blocks + xref_block, -1)
    first = (lax.axis_index("seq") // 2) * 2 * blocks
    meta = jnp.concatenate([
        jnp.pad(target, ((0, 0), (0, 128 - xrefs))),
        block_section[None, :],
        jnp.pad(section_parent, (0, 128 - section_parent.shape[0]))[None, :],
        jnp.full((2, 128), first, jnp.int32),
    ], axis=0)
    qh, kall, vall, wall, d_attn, metas = gather(queries, keys, values, out_weight.T, d_proj, meta, seq)
    attn, dq, dk, dv = attention(metas.reshape(16, 128), qh, kall, vall, d_attn)
    return scatter(dk, dv, attn, wall, dq, d_proj.shape[1])


def solution(mesh):
    split = P("seq", "head")
    rows = P("seq", None)
    return jax.shard_map(
        on_device, mesh=mesh,
        in_specs=(split, split, split, P("head", "seq"), split, P(), P(), rows, rows, rows),
        out_specs=(split,) * 4, check_vma=False)
```

time: 880 us -> 235 us (0.27); the launches traced: 870 us -> 235 us
  local copies, waits for them, and re-layouts: 324 us -> 17 us
  waiting for transfers between devices: 245 us -> 0 us
  matrix products: 220 us -> 0 us
  Pallas kernels: 0 us -> 215 us
  starting transfers between devices: 37.2 us -> 0 us
  blocking collectives: 16.2 us -> 0 us
  between operations: 16.7 us -> 0.71 us
    pallas_call x0 -> x3, Pallas kernels: none -> 215 us  [the longest x1 79.4 us: attention(): pl.pallas_call(functools.partial(attention_kernel, NBLK, NSEC, NQ, G, XR)...]
    psum x2 -> x0, waiting for transfers between devices: 183 us -> none  [the longest x1 99.5 us: on_device(): lax.psum(section_dk.astype(jnp.bfloat16), 'seq').astype(jnp.float32)]
    dot_general x38 -> x0, matrix products: 145 us -> none  [the longest x20 89.6 us: product(): return jnp.einsum(form, left, right, preferred_element_type=jnp.float32)]
    reshape x34 -> x0, local copies, waits for them, and re-layouts: 79.8 us -> none  [the longest x20 14.5 us: key_layout(): return key_set.reshape(num_blocks * row_count, kv_heads, HEAD_DIMENSION)]
    sub x8 -> x0, matrix products: 75.3 us -> none  [softmax_weights(): exponent = jnp.where(allowed, jnp.exp(masked - row_max), 0.0)]
    all_to_all x4 -> x0, waiting for transfers between devices: 61.2 us -> none  [the longest x1 37.1 us: on_device(): lax.all_to_all(out_keys, 'seq', split_axis=0, concat_axis=0, tiled=True)]
    broadcast_in_dim x18 -> x2, local copies, waits for them, and re-layouts: 44.6 us -> 0.66 us  [the longest x1 0.66 us: on_device(): jnp.pad(section_parent, (0, 128 - section_parent.shape[0]))[None, :]]
    dynamic_slice x34 -> x0, local copies, waits for them, and re-layouts: 38.4 us -> none  [the longest x32 37.6 us: on_device(): lax.map(run_forward, (query_blocks, key_sets, value_sets, allowed))]
  transfers between devices with their start and end apart: 13 -> 0, of which waited for: 4 -> 0; matrix products, arithmetic and copies ran while one was open for 27% -> 0% of each run, Pallas kernels for 0% -> 0%
where the time goes in v1:
time: 235 us
  Pallas kernels  215 us (91%)
  local copies, waits for them, and re-layouts  17 us (7%)
    pallas_call x1, Pallas kernels, attention(): pl.pallas_call(functools.partial(attention_kernel, NBLK, NSEC, NQ, G, XR)...  79.4 us
    pallas_call x1, Pallas kernels, gather(): pl.pallas_call(gather_kernel, out_shape=(jax.ShapeDtypeStruct((2 * T, W),...  76.2 us
    pallas_call x1, Pallas kernels, scatter(): pl.pallas_call(scatter_kernel, out_shape=(jax.ShapeDtypeStruct((T, D), BF...  59.6 us
    unnamed x30, local copies, waits for them, and re-layouts  16.2 us

profile of v1, /device:TPU:1, one launch (start us, length us, event | category | flops | bytes accessed | tf_op | source)
XLA Modules:
  0.0 234.9 jit_solution(8007972495310619889)
XLA Ops:
  0.7 0.1 pad.13.clone
  0.7 0.7 pad_bitcast_fusion
  1.4 0.7 multiply_reduce_fusion
  2.1 0.1 mul.15
  2.1 0.7 add_select_fusion
  2.8 0.7 fusion.1.meta
  3.6 0.0 copy-start.1
  3.6 1.3 copy-done.1
  4.9 0.0 copy-start.2
  4.9 1.1 copy-done.2
  6.0 0.0 copy-start.3
  6.0 0.9 copy-done.3
  6.9 0.0 copy-start.4
  6.9 0.9 copy-done.4
  7.9 0.0 copy-start.5
  7.9 0.9 copy-done.5
  8.8 76.2 %shard_map.129 = (bf16[1024,640]{1,0:T(8,128)(2,1)S(1)}, bf16[16384,128]{1,0:T(8,128)(2,1)S(1)}, bf16[16384,128]{1,0:T(8,128)(2,1)}, bf16[2560,640]{1,0:T(8,128)...) custom-call(bf16[512,1280]{1,0:T(8,128)(2,1)S(1)} %copy-done.1, bf16[512,256]{1,0:T(8,128)(2,1)S(1)} %copy-done.3, ...), custom_call_target="tpu_custom_call" | custom-call | flops 3400000000 | bytes 40000000 | tf_op jit(solution)/shard_map/pallas_call | solution.py:493
  85.0 0.0 copy-start
  85.0 1.7 copy-done
  86.7 0.0 copy-start.6
  86.7 0.6 copy-done.6
  87.3 0.0 copy-start.7
  87.3 1.9 copy-done.7
  89.2 0.0 copy-start.8
  89.2 1.1 copy-done.8
  90.3 0.0 copy-start.9
  90.3 1.1 copy-done.9
  91.4 79.4 %shard_map.130 = (bf16[1024,640]{1,0:T(8,128)(2,1)}, bf16[1024,640]{1,0:T(8,128)(2,1)}, bf16[16384,128]{1,0:T(8,128)(2,1)}, bf16[16384,128]{1,0:T(8,128)(2,1)}) custom-call(s32[16,128]{1,0:T(8,128)} %bitcast.6, bf16[1024,640]{1,0:T(8,128)(2,1)} %copy-done.8, bf16[16384,128]{1,0:T(8,128)(2,1)} %copy-done.7, bf16[16384,128]{1,0:T(8,128)(2,1)} %get-tuple-element.17.v_hbm, ...), custom_call_target="tpu_custom_call" | custom-call | flops 17999998976 | bytes 24000000 | tf_op jit(solution)/shard_map/pallas_call | solution.py:215
  170.7 59.6 %shard_map.131 = (bf16[512,640]{1,0:T(8,128)(2,1)}, bf16[512,1280]{1,0:T(8,128)(2,1)}, bf16[512,256]{1,0:T(8,128)(2,1)}, bf16[512,256]{1,0:T(8,128)(2,1)}) custom-call(bf16[16384,128]{1,0:T(8,128)(2,1)} %get-tuple-element.19.dk, bf16[16384,128]{1,0:T(8,128)(2,1)} %get-tuple-element.20.dv, bf16[1024,640]{1,0:T(8,128)(2,1)} %get-tuple-element.21.attn, ...), custom_call_target="tpu_custom_call" | custom-call | flops 3400000000 | bytes 40000000 | tf_op jit(solution)/shard_map/pallas_call | solution.py:700
  230.3 0.0 copy-start.10
  230.3 2.1 copy.18
  232.4 0.0 copy-done.10
  232.4 0.0 copy-start.12
  232.4 0.0 copy-start.11
  232.4 1.1 copy.19
  233.5 0.0 copy-done.12
  233.5 0.7 copy.20
  234.2 0.0 copy-done.11
  234.2 0.7 copy.21
  (1 shorter events, 0.0 us)
Async XLA Ops:
  3.6 1.3 copy-start.1
  4.9 1.1 copy-start.2
  6.0 0.9 copy-start.3
  6.9 0.9 copy-start.4
  7.9 0.9 copy-start.5
  85.0 1.7 copy-start
  86.7 0.6 copy-start.6
  87.3 1.9 copy-start.7
  89.2 1.1 copy-start.8
  90.3 1.1 copy-start.9
  230.3 2.1 copy-start.10
  232.4 1.1 copy-start.12
  232.4 1.8 copy-start.11

commit v2 on v1

--- a/solution.py
+++ b/solution.py
@@ -11,44 +11,48 @@
 
 HD = 128
 BLK = 128
-LOG2E = 1.4426950408889634
-
-
-def attention_kernel(NBLK, NSEC, NQ, G, XR, meta, q_ref, k_hbm, v_hbm, do_ref, attn_ref, dq_ref, dk_ref, dv_ref,
-                     kc, vc, ak, av, sbuf, qs, dos, dot_t, ot, mrun, lrun, slots, counts, first, length, sems):
+CHUNK = 4
+BOTH = 2
+
+
+def attention_kernel(NBLK, NSEC, NQ, G, XR, meta, q_hbm, k_hbm, v_hbm, do_hbm, attn_hbm, dq_hbm, dk_hbm, dv_hbm,
+                     kc, vc, ak, av, sbuf0, sbuf1, q_ref, do_ref, attn_ref, dq_ref, dk_ref, dv_ref,
+                     qs_t, dot_t, ot0, ot1, shares, slots, counts, first, stop, done, sems):
     scaling = HD ** -0.5
+    sbuf, ot = (sbuf0, sbuf1), (ot0, ot1)
     NT = (((1,), (1,)), ((), ()))
     TN = (((0,), (0,)), ((), ()))
     NN = (((1,), (0,)), ((), ()))
+    R = CHUNK * BLK
 
     def mm(a, b, dims):
         return lax.dot_general(a, b, dims, preferred_element_type=F32)
 
-    load_k = pltpu.make_async_copy(k_hbm, kc.at[pl.ds(0, NBLK * BLK)], sems.at[0])
-    load_v = pltpu.make_async_copy(v_hbm, vc.at[pl.ds(0, NBLK * BLK)], sems.at[1])
-    load_k.start()
-    load_v.start()
+    loads = [pltpu.make_async_copy(src, dst, sems.at[i]) for i, (src, dst) in enumerate((
+        (k_hbm, kc.at[pl.ds(0, NBLK * BLK)]), (v_hbm, vc.at[pl.ds(0, NBLK * BLK)]), (q_hbm, q_ref), (do_hbm, do_ref)))]
+    for copy in loads:
+        copy.start()
 
     @pl.loop(0, NSEC)
     def _(s):
-        length[s] = 0
+        stop[s] = 0
         first[s] = 0
-
-    @pl.loop(0, NBLK)
-    def _(c):
-        s = meta[4, c]
-        n = length[s]
-
-        @pl.when(n == 0)
-        def _():
-            first[s] = c
-        length[s] = n + 1
+        done[s] = 0
+
+    @pl.loop(0, NBLK // 8)
+    def _(i):
+        for h in range(8):
+            c = i * 8 + h
+            stop[meta[4, c]] = c + 1
+            d = NBLK - 1 - c
+            first[meta[4, d]] = d
 
     @pl.loop(0, NQ)
     def _(b):
         g = meta[6, 0] + b
         mine = meta[4, g]
-        slots[b, 0] = g
+        for j in range(32):
+            slots[b, j] = g
         slots[b, 1] = NBLK + mine
         n = jnp.int32(2)
         for w in (1, 2, 3):
@@ -64,6 +68,7 @@
             t = meta[row, j]
             slots[b, n] = jnp.maximum(t, 0) + 256
             n = n + jnp.where(t >= 0, 1, 0)
+        slots[b, n] = g
         counts[b] = n
 
     @pl.loop(0, (NBLK + NSEC) // 4)
@@ -72,137 +77,169 @@
         ak[at, :] = jnp.zeros((512, HD), F32)
         av[at, :] = jnp.zeros((512, HD), F32)
 
-    load_k.wait()
-    load_v.wait()
-
-    def block(ref, i):
-        return ref[pl.ds(pl.multiple_of(i * BLK, BLK), BLK), :]
-
-    def root(s):
-        return jnp.sqrt(jnp.full((8, HD), jnp.maximum(length[s], 1)).astype(F32))[:1]
-
+    for copy in loads:
+        copy.wait()
+
+    def span(i):
+        return pl.ds(pl.multiple_of(i * BLK, BLK), BLK)
+
+    def summarize(s):
+        def add(c, t):
+            return t[0] + kc[span(c), :].astype(F32), t[1] + vc[span(c), :].astype(F32)
+        zero = jnp.zeros((BLK, HD), F32)
+        tk, tv = lax.fori_loop(first[s], stop[s], add, (zero, zero))
+        share = 1.0 / jnp.sqrt(jnp.full((8, HD), jnp.maximum(stop[s] - first[s], 1)).astype(F32))
+        shares[s] = share
+        kc[span(NBLK + s), :] = (tk * share[:1]).astype(BF)
+        vc[span(NBLK + s), :] = (tv * share[:1]).astype(BF)
+        done[s] = 1
+
+    @pl.loop(0, 2 * NQ)
+    def _(i):
+        mine = meta[4, meta[6, 0] + lax.div(i, 2)]
+        s = jnp.where(lax.rem(i, 2) == 0, mine, jnp.maximum(meta[5, mine], 0))
+
+        @pl.when(done[s] == 0)
+        def _():
+            summarize(s)
+
+    W = G * BLK
+    row_id = lax.broadcasted_iota(jnp.int32, (BLK, BLK), 0)
+    col_id = lax.broadcasted_iota(jnp.int32, (BLK, BLK), 1)
+    causal = jnp.concatenate([row_id <= col_id] * G, axis=1)
+
+    def fold(op, s):
+        return op(s.reshape(s.shape[0] // 8, 8, W), axis=0)
+
+    ones = jnp.ones((R, 16), BF)
+
+    TWO = range(BOTH)
+
+    @pl.loop(0, NQ // BOTH)
+    def _(u):
+        bs = [u * BOTH + t for t in TWO]
+        bases = [pl.multiple_of(b * BLK, BLK) for b in bs]
+        for t in TWO:
+            for g in range(G):
+                part = slice(g * BLK, (g + 1) * BLK)
+                qs_t[t, :, part] = q_ref[pl.ds(bases[t], BLK), part].astype(F32).T.astype(BF)
+                dot_t[t, :, part] = do_ref[pl.ds(bases[t], BLK), part].astype(F32).T.astype(BF)
+        ns = [counts[b] for b in bs]
+        most = ns[0]
+        for n in ns[1:]:
+            most = jnp.maximum(most, n)
+        chunks = lax.div(most + CHUNK - 1, CHUNK)
+
+        def chunk(t, ref, j):
+            return jnp.concatenate([ref[span(slots[bs[t], CHUNK * j + h] & 255), :] for h in range(CHUNK)], axis=0)
+
+        def rows(j):
+            return pl.ds(pl.multiple_of(j * R, R), R)
+
+        def scores(t, j):
+            s = mm(chunk(t, kc, j), qs_t[t], NN) * scaling
+            return jnp.concatenate([
+                s[h * BLK:(h + 1) * BLK] + jnp.where(CHUNK * j + h < ns[t], 0.0, -1e30) for h in range(CHUNK)], axis=0)
+
+        tops = []
+        for t in TWO:
+            s0 = scores(t, 0)
+            s0 = jnp.concatenate([jnp.where(causal, s0[:BLK], -1e30), s0[BLK:]], axis=0)
+            sbuf[t][rows(0), :] = s0
+            tops.append(fold(jnp.max, s0))
+
+        def score(j, ms):
+            ss = [scores(t, j) for t in TWO]
+            for t in TWO:
+                sbuf[t][rows(j), :] = ss[t]
+            return tuple(jnp.maximum(ms[t], fold(jnp.max, ss[t])) for t in TWO)
+        tops = lax.fori_loop(1, chunks, score, tuple(tops))
+        tops = [jnp.max(m, axis=0, keepdims=True) for m in tops]
+
+        for t in TWO:
+            ot[t][...] = jnp.zeros((HD + 16, W), F32)
+
+        def forward(j, carry):
+            es = [jnp.exp(sbuf[t][rows(j), :] - tops[t]) for t in TWO]
+            for t in TWO:
+                sbuf[t][rows(j), :] = es[t]
+            for t in TWO:
+                ot[t][...] += mm(jnp.concatenate([chunk(t, vc, j), ones], axis=1), es[t].astype(BF), TN)
+            return carry
+        lax.fori_loop(0, chunks, forward, 0)
+        rls, deltas = [], []
+        for t in TWO:
+            rl = 1.0 / ot[t][HD:HD + 1, :]
+            o_t = (ot[t][:HD, :] * rl).astype(BF).astype(F32)
+            rls.append(rl)
+            deltas.append(jnp.sum(o_t * dot_t[t].astype(F32), axis=0, keepdims=True))
+            for g in range(G):
+                part = slice(g * BLK, (g + 1) * BLK)
+                attn_ref[pl.ds(bases[t], BLK), part] = o_t[:, part].T.astype(BF)
+
+        def put(acc, t, i, term):
+            slot = slots[bs[t], i]
+            where = span(slot & 255)
+            acc[where, :] += jnp.where(slot >= 256, term.astype(BF).astype(F32), term)
+
+        for t in TWO:
+            ot[t][:HD, :] = jnp.zeros((HD, W), F32)
+
+        def backward(j, carry):
+            terms = []
+            for t in TWO:
+                k, v = chunk(t, kc, j), chunk(t, vc, j)
+                p = sbuf[t][rows(j), :] * rls[t]
+                ds = (p * (mm(v, dot_t[t], NN) - deltas[t])).astype(BF)
+                dv = mm(dot_t[t], p.astype(BF), NT)
+                dk = mm(qs_t[t], ds, NT) * scaling
+                ot[t][:HD, :] += mm(k, ds, TN)
+                terms.append((dk, dv))
+            for t in TWO:
+                dk, dv = terms[t]
+                for h in range(CHUNK):
+                    put(ak, t, CHUNK * j + h, dk[:, h * BLK:(h + 1) * BLK])
+                    put(av, t, CHUNK * j + h, dv[:, h * BLK:(h + 1) * BLK])
+            return carry
+        lax.fori_loop(0, chunks, backward, 0)
+        for t in TWO:
+            for g in range(G):
+                part = slice(g * BLK, (g + 1) * BLK)
+                dq_ref[pl.ds(bases[t], BLK), part] = (ot[t][:HD, part] * scaling).T.astype(BF)
+
+    saves = [pltpu.make_async_copy(attn_ref, attn_hbm, sems.at[4]), pltpu.make_async_copy(dq_ref, dq_hbm, sems.at[5])]
+    for copy in saves:
+        copy.start()
     @pl.loop(0, NSEC)
     def _(s):
-        for ref in (kc, vc):
-            total = lax.fori_loop(first[s], first[s] + length[s],
-                                  lambda c, t: t + block(ref, c).astype(F32), jnp.zeros((BLK, HD), F32))
-            ref[pl.ds(pl.multiple_of((NBLK + s) * BLK, BLK), BLK), :] = (total / root(s)).astype(BF)
-
-    W = G * BLK
-    row_id = lax.broadcasted_iota(jnp.int32, (2 * BLK, BLK), 0)
-    col_id = lax.broadcasted_iota(jnp.int32, (2 * BLK, BLK), 1)
-    open_one = (row_id <= col_id) | (row_id >= BLK)
-    open_all = jnp.concatenate([open_one] * G, axis=1)
-    c2 = scaling * LOG2E
-
-    def fold(op, s):
-        return op(s.reshape(s.shape[0] // 8, 8, W), axis=0)
-
-    @pl.loop(0, NQ)
-    def _(b):
-        base = pl.multiple_of(b * BLK, BLK)
-        for g in range(G):
-            part = slice(g * BLK, (g + 1) * BLK)
-            qs[part, :] = q_ref[pl.ds(base, BLK), part]
-            d = do_ref[pl.ds(base, BLK), part]
-            dos[part, :] = d
-            dot_t[:, part] = d.astype(F32).T.astype(BF)
-        n = counts[b]
-        pairs = lax.div(n, 2)
-        odd = lax.rem(n, 2) == 1
-
-        def idx(i):
-            return slots[b, i] & 255
-
-        def pair(ref, j):
-            return jnp.concatenate([block(ref, idx(2 * j)), block(ref, idx(2 * j + 1))], axis=0)
-
-        def at2(j):
-            return pl.ds(pl.multiple_of(j * 2 * BLK, 2 * BLK), 2 * BLK)
-
-        last = pl.ds(pl.multiple_of((n - 1) * BLK, BLK), BLK)
-
-        s0 = jnp.where(open_all, mm(pair(kc, 0), qs[...], NT), -1e30)
-        sbuf[at2(0), :] = s0
-
-        def score(j, m):
-            s = mm(pair(kc, j), qs[...], NT)
-            sbuf[at2(j), :] = s
-            return jnp.maximum(m, fold(jnp.max, s))
-        mrun[...] = lax.fori_loop(1, pairs, score, fold(jnp.max, s0))
-
-        @pl.when(odd)
+        @pl.when(done[s] == 1)
         def _():
-            s = mm(block(kc, idx(n - 1)), qs[...], NT)
-            sbuf[last, :] = s
-            mrun[...] = jnp.maximum(mrun[...], fold(jnp.max, s))
-        top = jnp.max(mrun[...], axis=0, keepdims=True) * c2
-
-        def weigh(rows, v):
-            e = jnp.exp2(sbuf[rows, :] * c2 - top)
-            sbuf[rows, :] = e
-            return fold(jnp.sum, e), mm(v, e.astype(BF), TN)
-
-        lrun[...], ot[...] = weigh(at2(0), pair(vc, 0))
-
-        def forward(j, l):
-            dl, o = weigh(at2(j), pair(vc, j))
-            ot[...] += o
-            return l + dl
-        lrun[...] = lax.fori_loop(1, pairs, forward, lrun[...])
-
-        @pl.when(odd)
-        def _():
-            dl, o = weigh(last, block(vc, idx(n - 1)))
-            ot[...] += o
-            lrun[...] += dl
-        rl = 1.0 / jnp.sum(lrun[...], axis=0, keepdims=True)
-        o_t = (ot[...] * rl).astype(BF).astype(F32)
-        delta = jnp.sum(o_t * dot_t[...].astype(F32), axis=0, keepdims=True) * scaling
-        for g in range(G):
-            part = slice(g * BLK, (g + 1) * BLK)
-            attn_ref[pl.ds(base, BLK), part] = o_t[:, part].T.astype(BF)
-
-        def put(acc, i, term):
-            slot = slots[b, i]
-            where = pl.ds(pl.multiple_of((slot & 255) * BLK, BLK), BLK)
-            term = jnp.where(slot >= 256, term.astype(BF).astype(F32), term)
-            acc[where, :] += term
-
-        def back(rows, k, v):
-            p = sbuf[rows, :] * rl
-            dp = mm(v, dot_t[...], NN)
-            ds = (p * (dp * scaling - delta)).astype(BF)
-            return mm(ds, qs[...], NN), mm(p.astype(BF), dos[...], NN), mm(k, ds, TN)
-
-        ot[...] = jnp.zeros((HD, W), F32)
-
-        def backward(j, carry):
-            dk, dv, dq = back(at2(j), pair(kc, j), pair(vc, j))
-            for h in range(2):
-                put(ak, 2 * j + h, dk[h * BLK:(h + 1) * BLK])
-                put(av, 2 * j + h, dv[h * BLK:(h + 1) * BLK])
-            ot[...] += dq
-            return carry
-        lax.fori_loop(0, pairs, backward, 0)
-
-        @pl.when(odd)
-        def _():
-            dk, dv, dq = back(last, block(kc, idx(n - 1)), block(vc, idx(n - 1)))
-            put(ak, n - 1, dk)
-            put(av, n - 1, dv)
-            ot[...] += dq
-        for g in range(G):
-            part = slice(g * BLK, (g + 1) * BLK)
-            dq_ref[pl.ds(base, BLK), part] = ot[:, part].T.astype(BF)
-
-    @pl.loop(0, NBLK)
-    def _(c):
-        s = meta[4, c]
-        share = 1.0 / root(s)
-        at = pl.ds(pl.multiple_of(c * BLK, BLK), BLK)
-        dk_ref[at, :] = (ak[at, :] + block(ak, NBLK + s) * share).astype(BF)
-        dv_ref[at, :] = (av[at, :] + block(av, NBLK + s) * share).astype(BF)
+            share = shares[s][:1]
+            gk, gv = ak[span(NBLK + s), :] * share, av[span(NBLK + s), :] * share
+
+            @pl.loop(first[s], stop[s])
+            def _(c):
+                ak[span(c), :] += gk
+                av[span(c), :] += gv
+
+    STEP = 4
+    PARTS = 4
+
+    for part in range(PARTS):
+        size = NBLK // PARTS
+
+        @pl.loop(part * size // STEP, (part + 1) * size // STEP)
+        def _(i):
+            at = pl.ds(pl.multiple_of(i * STEP * BLK, STEP * BLK), STEP * BLK)
+            dk_ref[at, :] = ak[at, :].astype(BF)
+            dv_ref[at, :] = av[at, :].astype(BF)
+        at = pl.ds(part * size * BLK, size * BLK)
+        for j, (src, dst) in enumerate(((dk_ref, dk_hbm), (dv_ref, dv_hbm))):
+            copy = pltpu.make_async_copy(src.at[at, :], dst.at[at, :], sems.at[6 + 2 * part + j])
+            copy.start()
+            saves.append(copy)
+    for copy in saves:
+        copy.wait()
 
 
 def attention(meta, q, k, v, do, NSEC=16, XR=12):
@@ -210,34 +247,41 @@
     NQ = q.shape[0] // BLK
     G = q.shape[1] // HD
     W = G * BLK
-    slots_most = 6 + XR
-    vm = pl.BlockSpec(memory_space=pltpu.VMEM)
+    slots_most = -(-(6 + XR) // CHUNK) * CHUNK
+    hbm = pl.BlockSpec(memory_space=pltpu.HBM)
+    every = ((NBLK + NSEC) * BLK, HD)
     return pl.pallas_call(
         functools.partial(attention_kernel, NBLK, NSEC, NQ, G, XR),
         out_shape=(jax.ShapeDtypeStruct(q.shape, BF), jax.ShapeDtypeStruct(q.shape, BF),
                    jax.ShapeDtypeStruct(k.shape, BF), jax.ShapeDtypeStruct(k.shape, BF)),
-        in_specs=[pl.BlockSpec(memory_space=pltpu.SMEM), vm, pl.BlockSpec(memory_space=pl.ANY),
-                  pl.BlockSpec(memory_space=pl.ANY), vm],
-        out_specs=(vm, vm, vm, vm),
+        in_specs=[pl.BlockSpec(memory_space=pltpu.SMEM)] + [hbm] * 4,
+        out_specs=(hbm,) * 4,
         scratch_shapes=[
-            pltpu.VMEM(((NBLK + NSEC) * BLK, HD), BF),
-            pltpu.VMEM(((NBLK + NSEC) * BLK, HD), BF),
-            pltpu.VMEM(((NBLK + NSEC) * BLK, HD), F32),
-            pltpu.VMEM(((NBLK + NSEC) * BLK, HD), F32),
+            pltpu.VMEM(every, BF),
+            pltpu.VMEM(every, BF),
+            pltpu.VMEM(every, F32),
+            pltpu.VMEM(every, F32),
             pltpu.VMEM((slots_most * BLK, W), F32),
-            pltpu.VMEM((W, HD), BF),
-            pltpu.VMEM((W, HD), BF),
-            pltpu.VMEM((HD, W), BF),
-            pltpu.VMEM((HD, W), F32),
-            pltpu.VMEM((8, W), F32),
-            pltpu.VMEM((8, W), F32),
-            pltpu.SMEM((NQ, 24), jnp.int32),
+            pltpu.VMEM((slots_most * BLK, W), F32),
+            pltpu.VMEM(q.shape, BF),
+            pltpu.VMEM(q.shape, BF),
+            pltpu.VMEM(q.shape, BF),
+            pltpu.VMEM(q.shape, BF),
+            pltpu.VMEM(k.shape, BF),
+            pltpu.VMEM(k.shape, BF),
+            pltpu.VMEM((BOTH, HD, W), BF),
+            pltpu.VMEM((BOTH, HD, W), BF),
+            pltpu.VMEM((HD + 16, W), F32),
+            pltpu.VMEM((HD + 16, W), F32),
+            pltpu.VMEM((NSEC, 8, HD), F32),
+            pltpu.SMEM((NQ, 32), jnp.int32),
             pltpu.SMEM((NQ,), jnp.int32),
             pltpu.SMEM((NSEC,), jnp.int32),
             pltpu.SMEM((NSEC,), jnp.int32),
-            pltpu.SemaphoreType.DMA((2,)),
+            pltpu.SMEM((NSEC,), jnp.int32),
+            pltpu.SemaphoreType.DMA((16,)),
         ],
-        compiler_params=pltpu.CompilerParams(vmem_limit_bytes=60 * 1024 * 1024),
+        compiler_params=pltpu.CompilerParams(vmem_limit_bytes=62 * 1024 * 1024),
         cost_estimate=pl.CostEstimate(flops=18_000_000_000, bytes_accessed=24_000_000, transcendentals=12_000_000),
     )(meta, q, k, v, do)
 
@@ -420,33 +464,30 @@
     gv.begin()
     w0.near()
     w1.near()
+    gk.near()
+    gv.near()
     w0.far()
     w1.far()
+    gk.far()
+    gv.far()
     L.arrived(ny[0], piece(L.c, 3))
     L.send(ny[2], piece(L.c, 3, 0), piece(L.c, 3, 0), "y", 1)
     L.arrived(ny[1], piece(L.c, 1))
     L.send(ny[3], piece(L.c, 1, 1), piece(L.c, 1, 1), "y", 3)
     L.send(nc[1], piece(L.c, 3), piece(L.c, 3), "c", 1)
     L.send(nc[2], piece(L.c, 1), piece(L.c, 1), "c", 1)
-    gk.near()
-    gv.near()
     for i in range(4):
         w0.relay(i)
         w1.relay(i)
-    gk.far()
-    gv.far()
+    for i in range(2):
+        gk.relay(i)
+        gv.relay(i)
     L.arrived(ny[2], piece(L.c, 2, 0))
     L.arrived(ny[3], piece(L.c, 2, 1))
     L.send(nc[3], piece(L.c, 2), piece(L.c, 2), "c", 1)
-    for i in range(2):
-        gk.relay(i)
-        gv.relay(i)
     for i in range(4):
         w0.end(i)
         w1.end(i)
-    own_d.wait()
-    for i, dy in enumerate((0, 3, 1, 2)):
-        L.arrived(nc[i], piece(other, dy))
     keep = pltpu.make_async_copy(wbuf, wall, own_sems.at[6])
     keep.start()
 
@@ -464,11 +505,15 @@
         def _(t):
             product(core, t)
 
-    products(0)
-    for i in range(2, 4):
-        gk.relay(i)
-        gv.relay(i)
-    products(1)
+    gk.relay(2)
+    gv.relay(2)
+    own_d.wait()
+    products(L.c)
+    gk.relay(3)
+    gv.relay(3)
+    for i, dy in enumerate((0, 3, 1, 2)):
+        L.arrived(nc[i], piece(other, dy))
+    products(other)
     save = pltpu.make_async_copy(abuf, dattn, own_sems.at[7])
     save.start()
     for i in range(4):
@@ -488,7 +533,7 @@
     W = q.shape[1] // 2
     C = wt.shape[0]
     D = dp.shape[1]
-    anywhere = pl.BlockSpec(memory_space=pl.ANY)
+    anywhere = pl.BlockSpec(memory_space=pltpu.HBM)
     sems = 128
     return pl.pallas_call(
         gather_kernel,
@@ -586,8 +631,10 @@
             self.L.arrived(self.na[2 + take], self.near2.at[take])
         for h in range(2):
             part = self.half(h)
-            self.final[part, :] = (self.total(3, 0, h) + self.near2[0, part, :].astype(F32)
-                                   + self.near2[1, part, :].astype(F32)).astype(BF)
+            value = (self.total(3, 0, h) + self.near2[0, part, :].astype(F32)
+                     + self.near2[1, part, :].astype(F32))
+            self.final[part, :] = jnp.concatenate(
+                [value[i:i + BLK].T for i in range(0, value.shape[0], BLK)], axis=0).astype(BF)
 
 
 def scatter_kernel(dk, dv, attn, wall, dq, proj, dqo, dko, dvo,
@@ -602,7 +649,7 @@
     L.barrier()
     sk = Scatter(L, dk, bufk, farr.at[0], nearr.at[0], far2.at[0], near2.at[0], final.at[0], "x", "z", own_sems.at[0])
     sv = Scatter(L, dv, bufv, farr.at[1], nearr.at[1], far2.at[1], near2.at[1], final.at[1], "z", "x", own_sems.at[1])
-    for i in range(4):
+    for i in range(2):
         sk.begin(i)
         sv.begin(i)
 
@@ -641,20 +688,26 @@
     sv.loaded()
     sk.pass_on(0)
     sv.pass_on(0)
+    sk.begin(2)
+    sv.begin(2)
     away(1)
     sk.pass_on(1)
     sv.pass_on(1)
+    sk.begin(3)
+    sv.begin(3)
     away(2)
+    sk.close(0)
+    sv.close(0)
     away(3)
     sk.pass_on(2)
     sv.pass_on(2)
     result[0] = mine(0).astype(BF)
     L.send(ny[0], result.at[0, pl.ds(0, mid), :], halves.at[0], "y", 1)
     L.send(ny[1], result.at[0, pl.ds(mid, mid), :], halves.at[1], "y", 3)
+    sk.close(1)
+    sv.close(1)
     sk.pass_on(3)
     sv.pass_on(3)
-    sk.close(0)
-    sv.close(0)
     value = mine(1)
     L.arrived(ny[0], halves.at[0])
     result[1] = jnp.concatenate([value[:mid] + halves[0].astype(F32), value[mid:]], axis=0).astype(BF)
@@ -663,9 +716,8 @@
     L.arrived(ny[1], halves.at[1])
     result[2] = jnp.concatenate([value[:mid], value[mid:] + halves[1].astype(F32)], axis=0).astype(BF)
     L.send(ny[3], result.at[2], wholes.at[1], "y", 3)
-    for i in (1, 2):
-        sk.close(i)
-        sv.close(i)
+    sk.close(2)
+    sv.close(2)
     value = mine(3)
     L.arrived(ny[2], wholes.at[0])
     L.arrived(ny[3], wholes.at[1])
@@ -694,7 +746,7 @@
     T = dq.shape[0] // 2
     W = dq.shape[1]
     HD = dk.shape[1]
-    anywhere = pl.BlockSpec(memory_space=pl.ANY)
+    anywhere = pl.BlockSpec(memory_space=pltpu.HBM)
     vmem = pl.BlockSpec(memory_space=pltpu.VMEM)
     sems = 64
     return pl.pallas_call(

time: 235 us -> 201 us (0.86)
  Pallas kernels: 215 us -> 181 us
    pallas_call x1, Pallas kernels: 79.4 us -> 52.4 us  [attention(): pl.pallas_call(functools.partial(attention_kernel, NBLK, NSEC, NQ, G, XR)...]
    pallas_call x1, Pallas kernels: 59.6 us -> 54.4 us  [scatter(): pl.pallas_call(scatter_kernel, out_shape=(jax.ShapeDtypeStruct((T, D), BF...]
where the time goes in v2:
time: 201 us
  Pallas kernels  181 us (90%)
  local copies, waits for them, and re-layouts  17 us (8%)
  other arithmetic  2.1 us (1%)
    pallas_call x1, Pallas kernels, gather(): pl.pallas_call(gather_kernel, out_shape=(jax.ShapeDtypeStruct((2 * T, W),...  74.1 us
    pallas_call x1, Pallas kernels, scatter(): pl.pallas_call(scatter_kernel, out_shape=(jax.ShapeDtypeStruct((T, D), BF...  54.4 us
    pallas_call x1, Pallas kernels, attention(): pl.pallas_call(functools.partial(attention_kernel, NBLK, NSEC, NQ, G, XR)...  52.4 us
    unnamed x30, local copies, waits for them, and re-layouts  16.2 us

profile of v2, /device:TPU:1, one launch (start us, length us, event | category | flops | bytes accessed | tf_op | source)
XLA Modules:
  0.0 200.7 jit_solution(10979985839627966738)
XLA Ops:
  0.7 0.1 pad.13.clone
  0.7 0.7 pad_bitcast_fusion
  1.4 0.7 multiply_reduce_fusion
  2.1 0.1 mul.15
  2.1 0.7 add_select_fusion
  2.8 0.7 fusion.1.meta
  3.6 0.0 copy-start.1
  3.6 1.3 copy-done.1
  4.9 0.0 copy-start.2
  4.9 1.1 copy-done.2
  6.0 0.0 copy-start.3
  6.0 0.9 copy-done.3
  6.9 0.0 copy-start.4
  6.9 0.9 copy-done.4
  7.9 0.0 copy-start.5
  7.9 0.9 copy-done.5
  8.8 74.1 %shard_map.129 = (bf16[1024,640]{1,0:T(8,128)(2,1)S(1)}, bf16[16384,128]{1,0:T(8,128)(2,1)S(1)}, bf16[16384,128]{1,0:T(8,128)(2,1)}, bf16[2560,640]{1,0:T(8,128)...) custom-call(bf16[512,1280]{1,0:T(8,128)(2,1)S(1)} %copy-done.1, bf16[512,256]{1,0:T(8,128)(2,1)S(1)} %copy-done.3, ...), custom_call_target="tpu_custom_call" | custom-call | flops 3400000000 | bytes 40000000 | tf_op jit(solution)/shard_map/pallas_call | solution.py:538
  82.9 0.0 copy-start
  82.9 1.7 copy-done
  84.6 0.0 copy-start.6
  84.6 0.6 copy-done.6
  85.2 0.0 copy-start.7
  85.2 1.9 copy-done.7
  87.1 0.0 copy-start.8
  87.1 1.1 copy-done.8
  88.2 0.0 copy-start.9
  88.2 1.1 copy-done.9
  89.3 52.4 %shard_map.130 = (bf16[1024,640]{1,0:T(8,128)(2,1)}, bf16[1024,640]{1,0:T(8,128)(2,1)}, bf16[16384,128]{1,0:T(8,128)(2,1)}, bf16[16384,128]{1,0:T(8,128)(2,1)}) custom-call(s32[16,128]{1,0:T(8,128)} %bitcast.6, bf16[1024,640]{1,0:T(8,128)(2,1)} %copy-done.8, bf16[16384,128]{1,0:T(8,128)(2,1)} %copy-done.7, bf16[16384,128]{1,0:T(8,128)(2,1)} %get-tuple-element.17.v_hbm, ...), custom_call_target="tpu_custom_call" | custom-call | flops 17999998976 | bytes 24000000 | tf_op jit(solution)/shard_map/pallas_call | solution.py:253
  141.7 54.4 %shard_map.131 = (bf16[512,640]{1,0:T(8,128)(2,1)}, bf16[512,1280]{1,0:T(8,128)(2,1)}, bf16[512,256]{1,0:T(8,128)(2,1)}, bf16[512,256]{1,0:T(8,128)(2,1)}) custom-call(bf16[16384,128]{1,0:T(8,128)(2,1)} %get-tuple-element.19.dk, bf16[16384,128]{1,0:T(8,128)(2,1)} %get-tuple-element.20.dv, bf16[1024,640]{1,0:T(8,128)(2,1)} %get-tuple-element.21.attn, ...), custom_call_target="tpu_custom_call" | custom-call | flops 3400000000 | bytes 40000000 | tf_op jit(solution)/shard_map/pallas_call | solution.py:752
  196.1 0.0 copy-start.10
  196.1 2.1 %copy.18 = bf16[512,640]{1,0:T(8,128)(2,1)} copy(bf16[512,640]{1,0:T(8,128)(2,1)} %get-tuple-element.28) | data formatting | bytes 1310720
  198.2 0.0 copy-done.10
  198.2 0.0 copy-start.12
  198.2 0.0 copy-start.11
  198.2 1.1 copy.19
  199.3 0.0 copy-done.12
  199.3 0.7 copy.20
  200.0 0.0 copy-done.11
  200.0 0.7 copy.21
  (1 shorter events, 0.0 us)
Async XLA Ops:
  3.6 1.3 copy-start.1
  4.9 1.1 copy-start.2
  6.0 0.9 copy-start.3
  6.9 0.9 copy-start.4
  7.9 0.9 copy-start.5
  82.9 1.7 copy-start
  84.6 0.6 copy-start.6
  85.2 1.9 copy-start.7
  87.1 1.1 copy-start.8
  88.2 1.1 copy-start.9
  196.1 2.1 %copy-start.10 = (bf16[512,1280]{1,0:T(8,128)(2,1)S(1)}, bf16[512,1280]{1,0:T(8,128)(2,1)}, u32[]{:S(2)}) copy-start(bf16[512,1280]{1,0:T(8,128)(2,1)} %get-tuple-element.29) | copy-start | bytes 3932164
  198.2 1.1 copy-start.12
  198.2 1.8 copy-start.11

commit v3 on v2

--- a/solution.py
+++ b/solution.py
@@ -15,9 +15,9 @@
 BOTH = 2
 
 
-def attention_kernel(NBLK, NSEC, NQ, G, XR, meta, q_hbm, k_hbm, v_hbm, do_hbm, attn_hbm, dq_hbm, dk_hbm, dv_hbm,
+def attention_kernel(NBLK, NSEC, NQ, G, XR, sec_hbm, par_hbm, xo_hbm, xb_hbm, xv_hbm, q_hbm, k_hbm, v_hbm, do_hbm, attn_hbm, dq_hbm, dk_hbm, dv_hbm,
                      kc, vc, ak, av, sbuf0, sbuf1, q_ref, do_ref, attn_ref, dq_ref, dk_ref, dv_ref,
-                     qs_t, dot_t, ot0, ot1, shares, slots, counts, first, stop, done, sems):
+                     qs_t, dot_t, ot0, ot1, shares, slots, counts, first, stop, done, sec, parent, xo, xb, xv, sems):
     scaling = HD ** -0.5
     sbuf, ot = (sbuf0, sbuf1), (ot0, ot1)
     NT = (((1,), (1,)), ((), ()))
@@ -30,8 +30,13 @@
 
     loads = [pltpu.make_async_copy(src, dst, sems.at[i]) for i, (src, dst) in enumerate((
         (k_hbm, kc.at[pl.ds(0, NBLK * BLK)]), (v_hbm, vc.at[pl.ds(0, NBLK * BLK)]), (q_hbm, q_ref), (do_hbm, do_ref)))]
-    for copy in loads:
+    tables = [pltpu.make_async_copy(src, dst, sems.at[16 + i]) for i, (src, dst) in enumerate((
+        (sec_hbm, sec), (par_hbm, parent), (xo_hbm, xo), (xb_hbm, xb), (xv_hbm, xv)))]
+    for copy in tables + loads:
         copy.start()
+    for copy in tables:
+        copy.wait()
+    begin = (lax.axis_index("seq") // 2) * NQ
 
     @pl.loop(0, NSEC)
     def _(s):
@@ -43,14 +48,14 @@
     def _(i):
         for h in range(8):
             c = i * 8 + h
-            stop[meta[4, c]] = c + 1
+            stop[sec[c]] = c + 1
             d = NBLK - 1 - c
-            first[meta[4, d]] = d
+            first[sec[d]] = d
 
     @pl.loop(0, NQ)
     def _(b):
-        g = meta[6, 0] + b
-        mine = meta[4, g]
+        g = begin + b
+        mine = sec[g]
         for j in range(32):
             slots[b, j] = g
         slots[b, 1] = NBLK + mine
@@ -59,15 +64,14 @@
             c = g - w
             cs = jnp.maximum(c, 0)
             slots[b, n] = cs
-            n = n + jnp.where((c >= 0) & (meta[4, cs] == mine), 1, 0)
-        up = meta[5, mine]
+            n = n + jnp.where((c >= 0) & (sec[cs] == mine), 1, 0)
+        up = parent[mine]
         slots[b, n] = NBLK + jnp.maximum(up, 0)
         n = n + jnp.where(up >= 0, 1, 0)
-        row = lax.div(b, 4) * 8 + lax.rem(b, 4)
+        core, row = lax.div(b, NQ // 2), lax.rem(b, NQ // 2)
         for j in range(XR):
-            t = meta[row, j]
-            slots[b, n] = jnp.maximum(t, 0) + 256
-            n = n + jnp.where(t >= 0, 1, 0)
+            slots[b, n] = xo[core, row * XR + j, 0] * (NQ // 2) + xb[core, row, j] + 256
+            n = n + jnp.where(xv[core, row, j] > 0, 1, 0)
         slots[b, n] = g
         counts[b] = n
 
@@ -96,8 +100,8 @@
 
     @pl.loop(0, 2 * NQ)
     def _(i):
-        mine = meta[4, meta[6, 0] + lax.div(i, 2)]
-        s = jnp.where(lax.rem(i, 2) == 0, mine, jnp.maximum(meta[5, mine], 0))
+        mine = sec[begin + lax.div(i, 2)]
+        s = jnp.where(lax.rem(i, 2) == 0, mine, jnp.maximum(parent[mine], 0))
 
         @pl.when(done[s] == 0)
         def _():
@@ -242,7 +246,9 @@
         copy.wait()
 
 
-def attention(meta, q, k, v, do, NSEC=16, XR=12):
+def attention(block_section, section_parent, xrefs, q, k, v, do):
+    NSEC = section_parent.shape[0]
+    XR = xrefs[1].shape[2]
     NBLK = k.shape[0] // BLK
     NQ = q.shape[0] // BLK
     G = q.shape[1] // HD
@@ -254,7 +260,7 @@
         functools.partial(attention_kernel, NBLK, NSEC, NQ, G, XR),
         out_shape=(jax.ShapeDtypeStruct(q.shape, BF), jax.ShapeDtypeStruct(q.shape, BF),
                    jax.ShapeDtypeStruct(k.shape, BF), jax.ShapeDtypeStruct(k.shape, BF)),
-        in_specs=[pl.BlockSpec(memory_space=pltpu.SMEM)] + [hbm] * 4,
+        in_specs=[hbm] * 9,
         out_specs=(hbm,) * 4,
         scratch_shapes=[
             pltpu.VMEM(every, BF),
@@ -279,11 +285,14 @@
             pltpu.SMEM((NSEC,), jnp.int32),
             pltpu.SMEM((NSEC,), jnp.int32),
             pltpu.SMEM((NSEC,), jnp.int32),
-            pltpu.SemaphoreType.DMA((16,)),
+            pltpu.SMEM(block_section.shape, jnp.int32),
+            pltpu.SMEM(section_parent.shape, jnp.int32),
+        ] + [pltpu.SMEM(a.shape, jnp.int32) for a in xrefs] + [
+            pltpu.SemaphoreType.DMA((24,)),
         ],
         compiler_params=pltpu.CompilerParams(vmem_limit_bytes=62 * 1024 * 1024),
         cost_estimate=pl.CostEstimate(flops=18_000_000_000, bytes_accessed=24_000_000, transcendentals=12_000_000),
-    )(meta, q, k, v, do)
+    )(block_section, section_parent, *xrefs, q, k, v, do)
 
 
 class Links:
@@ -395,7 +404,7 @@
         self.L.arrived(self.nb[i][3], self.at(da, 2, 1))
 
 
-def gather_kernel(q, k, v, wt, dp, meta, qh, kall, vall, wall, dattn, metas, wbuf, dbuf, abuf, send_sems, recv_sems, own_sems):
+def gather_kernel(q, k, v, wt, dp, xo, xb, xv, qh, kall, vall, wall, dattn, xos, xbs, xvs, wbuf, dbuf, abuf, send_sems, recv_sems, own_sems):
     L = Links(send_sems, recv_sems)
     chip = L.x * RING + L.z
     other = 1 - L.c
@@ -423,11 +432,13 @@
         copy = pltpu.make_async_copy(src.at[:, pl.ds(pl.multiple_of(L.c * width, 128), width)], at, own_sems.at[i])
         copy.start()
         own.append(copy)
-    n_meta = L.number()
-    mrow = metas.at[L.c]
-    L.send(n_meta, meta, mrow, "c", 1)
-    own_meta = pltpu.make_async_copy(meta, mrow, own_sems.at[4])
-    own_meta.start()
+    refs = []
+    for i, (src, dst) in enumerate(((xo, xos), (xb, xbs), (xv, xvs))):
+        n = L.number()
+        L.send(n, src, dst.at[L.c], "c", 1)
+        copy = pltpu.make_async_copy(src, dst.at[L.c], own_sems.at[8 + i])
+        copy.start()
+        refs.append((n, dst, copy))
 
     def piece(core, dy, half=None):
         ref = dbuf.at[core * RING + (L.y + dy) % RING]
@@ -520,14 +531,15 @@
         gk.end(i)
         gv.end(i)
     both(3)
-    L.arrived(n_meta, metas.at[other])
-    own_meta.wait()
+    for n, dst, copy in refs:
+        L.arrived(n, dst.at[other])
+        copy.wait()
     keep.wait()
     save.wait()
     L.finish()
 
 
-def gather(q, k, v, wt, dp, meta, seq):
+def gather(q, k, v, wt, dp, xrefs, seq):
     T = k.shape[0]
     HD = k.shape[1] // 2
     W = q.shape[1] // 2
@@ -543,22 +555,21 @@
             jax.ShapeDtypeStruct((seq * T, HD), BF),
             jax.ShapeDtypeStruct((seq * C, W), BF),
             jax.ShapeDtypeStruct((2 * T, W), BF),
-            jax.ShapeDtypeStruct((2,) + meta.shape, jnp.int32),
-        ),
-        in_specs=[anywhere] * 6,
-        out_specs=(anywhere,) * 6,
+        ) + tuple(jax.ShapeDtypeStruct((2,) + a.shape, jnp.int32) for a in xrefs),
+        in_specs=[anywhere] * 8,
+        out_specs=(anywhere,) * 8,
         scratch_shapes=[
             pltpu.VMEM((seq * C, W), BF),
             pltpu.VMEM((2 * RING, T, D), BF),
             pltpu.VMEM((2 * T, W), BF),
             pltpu.SemaphoreType.DMA((sems,)),
             pltpu.SemaphoreType.DMA((sems,)),
-            pltpu.SemaphoreType.DMA((8,)),
+            pltpu.SemaphoreType.DMA((11,)),
         ],
         compiler_params=pltpu.CompilerParams(
-            collective_id=0, has_side_effects=True, vmem_limit_bytes=40 * 1024 * 1024),
+            collective_id=0, has_side_effects=True, vmem_limit_bytes=62 * 1024 * 1024),
         cost_estimate=pl.CostEstimate(flops=3_400_000_000, bytes_accessed=40_000_000, transcendentals=0),
-    )(q, k, v, wt, dp, meta)
+    )(q, k, v, wt, dp, *xrefs)
 
 
 class Scatter:
@@ -777,25 +788,44 @@
             pltpu.SemaphoreType.DMA((6,)),
         ],
         compiler_params=pltpu.CompilerParams(
-            collective_id=1, has_side_effects=True, vmem_limit_bytes=56 * 1024 * 1024),
+            collective_id=1, has_side_effects=True, vmem_limit_bytes=62 * 1024 * 1024),
         cost_estimate=pl.CostEstimate(flops=3_400_000_000, bytes_accessed=40_000_000, transcendentals=0),
     )(dk, dv, attn, wall, dq)
 
 
+def hand_on_kernel(*refs):
+    count = (len(refs) - 1) // 2
+    sems = refs[-1]
+    copies = []
+    for src, dst in zip(refs[:count], refs[count:-1]):
+        rows = src.shape[0] // 4
+        for i in range(4):
+            part = pl.ds(i * rows, rows)
+            copies.append(pltpu.make_async_copy(src.at[part, :], dst.at[part, :], sems.at[len(copies)]))
+            copies[-1].start()
+    for copy in copies:
+        copy.wait()
+
+
+def hand_on(*arrays):
+    hbm = pl.BlockSpec(memory_space=pltpu.HBM)
+    return pl.pallas_call(
+        hand_on_kernel,
+        out_shape=tuple(jax.ShapeDtypeStruct(a.shape, a.dtype) for a in arrays),
+        in_specs=[hbm] * len(arrays),
+        out_specs=(hbm,) * len(arrays),
+        scratch_shapes=[pltpu.SemaphoreType.DMA((4 * len(arrays),))],
+        compiler_params=pltpu.CompilerParams(vmem_limit_bytes=62 * 1024 * 1024),
+        cost_estimate=pl.CostEstimate(flops=0, bytes_accessed=5_000_000, transcendentals=0),
+    )(*arrays)
+
+
 def on_device(queries, keys, values, out_weight, d_proj, block_section, section_parent, xref_owner, xref_block, xref_valid):
     seq = lax.axis_size("seq")
-    blocks, xrefs = xref_block.shape
-    target = jnp.where(xref_valid > 0, xref_owner.reshape(blocks, xrefs) * blocks + xref_block, -1)
-    first = (lax.axis_index("seq") // 2) * 2 * blocks
-    meta = jnp.concatenate([
-        jnp.pad(target, ((0, 0), (0, 128 - xrefs))),
-        block_section[None, :],
-        jnp.pad(section_parent, (0, 128 - section_parent.shape[0]))[None, :],
-        jnp.full((2, 128), first, jnp.int32),
-    ], axis=0)
-    qh, kall, vall, wall, d_attn, metas = gather(queries, keys, values, out_weight.T, d_proj, meta, seq)
-    attn, dq, dk, dv = attention(metas.reshape(16, 128), qh, kall, vall, d_attn)
-    return scatter(dk, dv, attn, wall, dq, d_proj.shape[1])
+    qh, kall, vall, wall, d_attn, *xrefs = gather(
+        queries, keys, values, out_weight.T, d_proj, (xref_owner, xref_block, xref_valid), seq)
+    attn, dq, dk, dv = attention(block_section, section_parent, xrefs, qh, kall, vall, d_attn)
+    return hand_on(*scatter(dk, dv, attn, wall, dq, d_proj.shape[1]))
 
 
 def solution(mesh):

time: 201 us -> 264 us (1.31)
  Pallas kernels: 181 us -> 262 us
  local copies, waits for them, and re-layouts: 17 us -> 1.35 us
    pallas_call x0 -> x1, Pallas kernels: none -> 76.7 us  [hand_on(): pl.pallas_call(hand_on_kernel, out_shape=tuple((jax.ShapeDtypeStruct(a.sh...]
    unnamed x30 -> x1, local copies, waits for them, and re-layouts: 16.2 us -> 1.35 us
    pallas_call x1, Pallas kernels: 74.1 us -> 76.8 us  [gather(): pl.pallas_call(gather_kernel, out_shape=(jax.ShapeDtypeStruct((2 * T, W),...]
where the time goes in v3:
time: 264 us
  Pallas kernels  262 us (99%)
    pallas_call x1, Pallas kernels, gather(): pl.pallas_call(gather_kernel, out_shape=(jax.ShapeDtypeStruct((2 * T, W),...  76.8 us
    pallas_call x1, Pallas kernels, hand_on(): pl.pallas_call(hand_on_kernel, out_shape=tuple((jax.ShapeDtypeStruct(a.sh...  76.7 us
    pallas_call x1, Pallas kernels, scatter(): pl.pallas_call(scatter_kernel, out_shape=(jax.ShapeDtypeStruct((T, D), BF...  56.1 us
    pallas_call x1, Pallas kernels, attention(): pl.pallas_call(functools.partial(attention_kernel, NBLK, NSEC, NQ, G, XR)...  51.9 us

profile of v3, /device:TPU:1, one launch (start us, length us, event | category | flops | bytes accessed | tf_op | source)
XLA Modules:
  0.0 263.7 jit_solution(3212809421611215710)
XLA Ops:
  0.6 1.3 copy.14.xo
  2.0 76.8 %shard_map.129 = (bf16[1024,640]{1,0:T(8,128)(2,1)}, bf16[16384,128]{1,0:T(8,128)(2,1)}, bf16[16384,128]{1,0:T(8,128)(2,1)}, bf16[2560,640]{1,0:T(8,128)(2,1)}, ...) custom-call(bf16[512,1280]{1,0:T(8,128)(2,1)} %q.1, ...), custom_call_target="tpu_custom_call" | custom-call | flops 3400000000 | bytes 40000000 | tf_op jit(solution)/shard_map/pallas_call | solution.py:550
  78.8 51.9 %shard_map.130 = (bf16[1024,640]{1,0:T(8,128)(2,1)}, bf16[1024,640]{1,0:T(8,128)(2,1)}, bf16[16384,128]{1,0:T(8,128)(2,1)}, bf16[16384,128]{1,0:T(8,128)(2,1)}) custom-call(s32[128]{0:T(128)} %sec_hbm.1, s32[16]{0:T(128)} %par_hbm.1, s32[2,48,1]{2,1,0:T(8,128)} %get-tuple-element.20.xo_hbm, s32[2,4,12]{2,1,0:T(4,128)} %get-tuple-element.21.xb_hbm, ...), custom_call_target="tpu_custom_call" | custom-call | flops 17999998976 | bytes 24000000 | tf_op jit(solution)/shard_map/pallas_call | solution.py:259
  130.8 56.1 %shard_map.131 = (bf16[512,640]{1,0:T(8,128)(2,1)}, bf16[512,1280]{1,0:T(8,128)(2,1)}, bf16[512,256]{1,0:T(8,128)(2,1)}, bf16[512,256]{1,0:T(8,128)(2,1)}) custom-call(bf16[16384,128]{1,0:T(8,128)(2,1)} %get-tuple-element.27.dk, bf16[16384,128]{1,0:T(8,128)(2,1)} %get-tuple-element.28.dv, bf16[1024,640]{1,0:T(8,128)(2,1)} %get-tuple-element.29.attn, ...), custom_call_target="tpu_custom_call" | custom-call | flops 3400000000 | bytes 40000000 | tf_op jit(solution)/shard_map/pallas_call | solution.py:763
  186.8 76.7 %shard_map.132 = (bf16[512,640]{1,0:T(8,128)(2,1)}, bf16[512,1280]{1,0:T(8,128)(2,1)}, bf16[512,256]{1,0:T(8,128)(2,1)}, bf16[512,256]{1,0:T(8,128)(2,1)}) custom-call(bf16[512,640]{1,0:T(8,128)(2,1)} %get-tuple-element.32.refs_0_, bf16[512,1280]{1,0:T(8,128)(2,1)} %get-tuple-element.33.refs_1_, bf16[512,256]{1,0:T(8,128)(2,1)} %get-tuple-element.34.refs_2_, ...), custom_call_target="tpu_custom_call" | custom-call | bytes 5000000 | tf_op jit(solution)/shard_map/pallas_call | solution.py:812

commit v4 on v3

--- a/solution.py
+++ b/solution.py
@@ -404,7 +404,7 @@
         self.L.arrived(self.nb[i][3], self.at(da, 2, 1))
 
 
-def gather_kernel(q, k, v, wt, dp, xo, xb, xv, qh, kall, vall, wall, dattn, xos, xbs, xvs, wbuf, dbuf, abuf, send_sems, recv_sems, own_sems):
+def gather_kernel(q_hbm, k_hbm, v_hbm, wt_hbm, dp_hbm, xo, xb, xv, qh, kall, vall, wall, dattn, xos, xbs, xvs, q, k, v, wt, dp, wbuf, dbuf, abuf, send_sems, recv_sems, own_sems):
     L = Links(send_sems, recv_sems)
     chip = L.x * RING + L.z
     other = 1 - L.c
@@ -413,7 +413,13 @@
     W = qh.shape[1]
     C = wt.shape[0]
     D = dp.shape[1]
+    loads = [pltpu.make_async_copy(src, dst, own_sems.at[11 + i]) for i, (src, dst) in enumerate((
+        (wt_hbm, wt), (k_hbm, k), (v_hbm, v), (dp_hbm, dp), (q_hbm, q)))]
+    for copy in loads:
+        copy.start()
     L.barrier()
+    for copy in loads:
+        copy.wait()
 
     pairs = []
 
@@ -558,13 +564,13 @@
         ) + tuple(jax.ShapeDtypeStruct((2,) + a.shape, jnp.int32) for a in xrefs),
         in_specs=[anywhere] * 8,
         out_specs=(anywhere,) * 8,
-        scratch_shapes=[
+        scratch_shapes=[pltpu.VMEM(a.shape, BF) for a in (q, k, v, wt, dp)] + [
             pltpu.VMEM((seq * C, W), BF),
             pltpu.VMEM((2 * RING, T, D), BF),
             pltpu.VMEM((2 * T, W), BF),
             pltpu.SemaphoreType.DMA((sems,)),
             pltpu.SemaphoreType.DMA((sems,)),
-            pltpu.SemaphoreType.DMA((11,)),
+            pltpu.SemaphoreType.DMA((16,)),
         ],
         compiler_params=pltpu.CompilerParams(
             collective_id=0, has_side_effects=True, vmem_limit_bytes=62 * 1024 * 1024),
@@ -648,8 +654,8 @@
                 [value[i:i + BLK].T for i in range(0, value.shape[0], BLK)], axis=0).astype(BF)
 
 
-def scatter_kernel(dk, dv, attn, wall, dq, proj, dqo, dko, dvo,
-                   bufk, bufv, farr, nearr, far2, near2, final, there, here, halves, wholes, result,
+def scatter_kernel(dk, dv, attn, wall, dq_hbm, proj, dqo, dko, dvo,
+                   dq, bufk, bufv, farr, nearr, far2, near2, final, there, here, halves, wholes, result,
                    send_sems, recv_sems, own_sems):
     L = Links(send_sems, recv_sems)
     other = 1 - L.c
@@ -657,6 +663,8 @@
     D = proj.shape[1]
     W = dq.shape[1]
     HD = dk.shape[1]
+    load_q = pltpu.make_async_copy(dq_hbm, dq, own_sems.at[6])
+    load_q.start()
     L.barrier()
     sk = Scatter(L, dk, bufk, farr.at[0], nearr.at[0], far2.at[0], near2.at[0], final.at[0], "x", "z", own_sems.at[0])
     sv = Scatter(L, dv, bufv, farr.at[1], nearr.at[1], far2.at[1], near2.at[1], final.at[1], "z", "x", own_sems.at[1])
@@ -670,6 +678,7 @@
     def heads(ref, core, width):
         return ref.at[:, pl.ds(pl.multiple_of(core * width, 128), width)]
 
+    load_q.wait()
     n_q = L.number()
     L.send(n_q, dq.at[rows_of(other), :], heads(dqo, L.c, W), "c", 1)
     own_q = pltpu.make_async_copy(dq.at[rows_of(L.c), :], heads(dqo, L.c, W), own_sems.at[2])
@@ -771,6 +780,7 @@
         in_specs=[anywhere, anywhere, vmem, vmem, anywhere],
         out_specs=(anywhere,) * 4,
         scratch_shapes=[
+            pltpu.VMEM(dq.shape, BF),
             pltpu.VMEM(dk.shape, BF),
             pltpu.VMEM(dk.shape, BF),
             pltpu.VMEM((2, 4, 2, T, HD), BF),
@@ -785,7 +795,7 @@
             pltpu.VMEM((4, T, D), BF),
             pltpu.SemaphoreType.DMA((sems,)),
             pltpu.SemaphoreType.DMA((sems,)),
-            pltpu.SemaphoreType.DMA((6,)),
+            pltpu.SemaphoreType.DMA((7,)),
         ],
         compiler_params=pltpu.CompilerParams(
             collective_id=1, has_side_effects=True, vmem_limit_bytes=62 * 1024 * 1024),
@@ -794,16 +804,21 @@
 
 
 def hand_on_kernel(*refs):
-    count = (len(refs) - 1) // 2
+    count = (len(refs) - 1) // 3
     sems = refs[-1]
-    copies = []
-    for src, dst in zip(refs[:count], refs[count:-1]):
-        rows = src.shape[0] // 4
-        for i in range(4):
+    inward, outward = [], []
+    for src, dst, held in zip(refs[:count], refs[count:2 * count], refs[2 * count:-1]):
+        rows = src.shape[0] // 2
+        for i in range(2):
             part = pl.ds(i * rows, rows)
-            copies.append(pltpu.make_async_copy(src.at[part, :], dst.at[part, :], sems.at[len(copies)]))
-            copies[-1].start()
-    for copy in copies:
+            n = len(inward)
+            inward.append(pltpu.make_async_copy(src.at[part, :], held.at[part, :], sems.at[0, n]))
+            outward.append(pltpu.make_async_copy(held.at[part, :], dst.at[part, :], sems.at[1, n]))
+            inward[-1].start()
+    for first, second in zip(inward, outward):
+        first.wait()
+        second.start()
+    for copy in outward:
         copy.wait()
 
 
@@ -814,7 +829,8 @@
         out_shape=tuple(jax.ShapeDtypeStruct(a.shape, a.dtype) for a in arrays),
         in_specs=[hbm] * len(arrays),
         out_specs=(hbm,) * len(arrays),
-        scratch_shapes=[pltpu.SemaphoreType.DMA((4 * len(arrays),))],
+        scratch_shapes=[pltpu.VMEM(a.shape, a.dtype) for a in arrays] + [
+            pltpu.SemaphoreType.DMA((2, 2 * len(arrays)))],
         compiler_params=pltpu.CompilerParams(vmem_limit_bytes=62 * 1024 * 1024),
         cost_estimate=pl.CostEstimate(flops=0, bytes_accessed=5_000_000, transcendentals=0),
     )(*arrays)

time: 264 us -> 188 us (0.71)
  Pallas kernels: 262 us -> 185 us
    pallas_call x1, Pallas kernels: 76.7 us -> 2.65 us  [hand_on(): pl.pallas_call(hand_on_kernel, out_shape=tuple((jax.ShapeDtypeStruct(a.sh...]
    pallas_call x1, Pallas kernels: 56.1 us -> 59.2 us  [scatter(): pl.pallas_call(scatter_kernel, out_shape=(jax.ShapeDtypeStruct((T, D), BF...]
where the time goes in v4:
time: 188 us
  Pallas kernels  185 us (98%)
    pallas_call x1, Pallas kernels, gather(): pl.pallas_call(gather_kernel, out_shape=(jax.ShapeDtypeStruct((2 * T, W),...  74.3 us
    pallas_call x1, Pallas kernels, scatter(): pl.pallas_call(scatter_kernel, out_shape=(jax.ShapeDtypeStruct((T, D), BF...  59.2 us
    pallas_call x1, Pallas kernels, attention(): pl.pallas_call(functools.partial(attention_kernel, NBLK, NSEC, NQ, G, XR)...  49.3 us

profile of v4, /device:TPU:1, one launch (start us, length us, event | category | flops | bytes accessed | tf_op | source)
XLA Modules:
  0.0 187.6 jit_solution(17577983147117657183)
XLA Ops:
  0.6 1.3 copy.14.xo
  2.0 74.3 %shard_map.129 = (bf16[1024,640]{1,0:T(8,128)(2,1)}, bf16[16384,128]{1,0:T(8,128)(2,1)}, bf16[16384,128]{1,0:T(8,128)(2,1)}, bf16[2560,640]{1,0:T(8,128)(2,1)}, ...) custom-call(bf16[512,1280]{1,0:T(8,128)(2,1)} %q_hbm.1, ...), custom_call_target="tpu_custom_call" | custom-call | flops 3400000000 | bytes 40000000 | tf_op jit(solution)/shard_map/pallas_call | solution.py:556
  76.3 49.3 %shard_map.130 = (bf16[1024,640]{1,0:T(8,128)(2,1)}, bf16[1024,640]{1,0:T(8,128)(2,1)}, bf16[16384,128]{1,0:T(8,128)(2,1)}, bf16[16384,128]{1,0:T(8,128)(2,1)}) custom-call(s32[128]{0:T(128)} %sec_hbm.1, s32[16]{0:T(128)} %par_hbm.1, s32[2,48,1]{2,1,0:T(8,128)} %get-tuple-element.20.xo_hbm, s32[2,4,12]{2,1,0:T(4,128)} %get-tuple-element.21.xb_hbm, ...), custom_call_target="tpu_custom_call" | custom-call | flops 17999998976 | bytes 24000000 | tf_op jit(solution)/shard_map/pallas_call | solution.py:259
  125.6 59.2 %shard_map.131 = (bf16[512,640]{1,0:T(8,128)(2,1)}, bf16[512,1280]{1,0:T(8,128)(2,1)}, bf16[512,256]{1,0:T(8,128)(2,1)}, bf16[512,256]{1,0:T(8,128)(2,1)}) custom-call(bf16[16384,128]{1,0:T(8,128)(2,1)} %get-tuple-element.27.dk, bf16[16384,128]{1,0:T(8,128)(2,1)} %get-tuple-element.28.dv, bf16[1024,640]{1,0:T(8,128)(2,1)} %get-tuple-element.29.attn, ...), custom_call_target="tpu_custom_call" | custom-call | flops 3400000000 | bytes 40000000 | tf_op jit(solution)/shard_map/pallas_call | solution.py:772
  184.8 2.6 %shard_map.132 = (bf16[512,640]{1,0:T(8,128)(2,1)}, bf16[512,1280]{1,0:T(8,128)(2,1)}, bf16[512,256]{1,0:T(8,128)(2,1)}, bf16[512,256]{1,0:T(8,128)(2,1)}) custom-call(bf16[512,640]{1,0:T(8,128)(2,1)} %get-tuple-element.32.refs_0_, bf16[512,1280]{1,0:T(8,128)(2,1)} %get-tuple-element.33.refs_1_, bf16[512,256]{1,0:T(8,128)(2,1)} %get-tuple-element.34.refs_2_, ...), custom_call_target="tpu_custom_call" | custom-call | bytes 5000000 | tf_op jit(solution)/shard_map/pallas_call | solution.py:827

commit v5 on v4

--- a/solution.py
+++ b/solution.py
@@ -17,7 +17,7 @@
 
 def attention_kernel(NBLK, NSEC, NQ, G, XR, sec_hbm, par_hbm, xo_hbm, xb_hbm, xv_hbm, q_hbm, k_hbm, v_hbm, do_hbm, attn_hbm, dq_hbm, dk_hbm, dv_hbm,
                      kc, vc, ak, av, sbuf0, sbuf1, q_ref, do_ref, attn_ref, dq_ref, dk_ref, dv_ref,
-                     qs_t, dot_t, ot0, ot1, shares, slots, counts, first, stop, done, sec, parent, xo, xb, xv, sems):
+                     qs_t, dot_t, ot0, ot1, shares, slots, counts, turn, first, stop, done, sec, parent, xo, xb, xv, sems):
     scaling = HD ** -0.5
     sbuf, ot = (sbuf0, sbuf1), (ot0, ot1)
     NT = (((1,), (1,)), ((), ()))
@@ -30,7 +30,7 @@
 
     loads = [pltpu.make_async_copy(src, dst, sems.at[i]) for i, (src, dst) in enumerate((
         (k_hbm, kc.at[pl.ds(0, NBLK * BLK)]), (v_hbm, vc.at[pl.ds(0, NBLK * BLK)]), (q_hbm, q_ref), (do_hbm, do_ref)))]
-    tables = [pltpu.make_async_copy(src, dst, sems.at[16 + i]) for i, (src, dst) in enumerate((
+    tables = [pltpu.make_async_copy(src, dst, sems.at[32 + i]) for i, (src, dst) in enumerate((
         (sec_hbm, sec), (par_hbm, parent), (xo_hbm, xo), (xb_hbm, xb), (xv_hbm, xv)))]
     for copy in tables + loads:
         copy.start()
@@ -70,10 +70,19 @@
         n = n + jnp.where(up >= 0, 1, 0)
         core, row = lax.div(b, NQ // 2), lax.rem(b, NQ // 2)
         for j in range(XR):
-            slots[b, n] = xo[core, row * XR + j, 0] * (NQ // 2) + xb[core, row, j] + 256
+            slots[b, n] = xo[core, 0, row * XR + j] * (NQ // 2) + xb[core, row, j] + 256
             n = n + jnp.where(xv[core, row, j] > 0, 1, 0)
         slots[b, n] = g
         counts[b] = n
+
+    for b in range(NQ):
+        place = jnp.int32(0)
+        for o in range(NQ):
+            if o < b:
+                place = place + jnp.where(counts[o] >= counts[b], 1, 0)
+            elif o > b:
+                place = place + jnp.where(counts[o] > counts[b], 1, 0)
+        turn[place] = b
 
     @pl.loop(0, (NBLK + NSEC) // 4)
     def _(i):
@@ -121,7 +130,7 @@
 
     @pl.loop(0, NQ // BOTH)
     def _(u):
-        bs = [u * BOTH + t for t in TWO]
+        bs = [turn[u * BOTH + t] for t in TWO]
         bases = [pl.multiple_of(b * BLK, BLK) for b in bs]
         for t in TWO:
             for g in range(G):
@@ -140,8 +149,10 @@
         def rows(j):
             return pl.ds(pl.multiple_of(j * R, R), R)
 
-        def scores(t, j):
+        def scores(t, j, full=False):
             s = mm(chunk(t, kc, j), qs_t[t], NN) * scaling
+            if full:
+                return s
             return jnp.concatenate([
                 s[h * BLK:(h + 1) * BLK] + jnp.where(CHUNK * j + h < ns[t], 0.0, -1e30) for h in range(CHUNK)], axis=0)
 
@@ -152,12 +163,17 @@
             sbuf[t][rows(0), :] = s0
             tops.append(fold(jnp.max, s0))
 
-        def score(j, ms):
-            ss = [scores(t, j) for t in TWO]
+        def score(full, j, ms):
+            ss = [scores(t, j, full) for t in TWO]
             for t in TWO:
                 sbuf[t][rows(j), :] = ss[t]
             return tuple(jnp.maximum(ms[t], fold(jnp.max, ss[t])) for t in TWO)
-        tops = lax.fori_loop(1, chunks, score, tuple(tops))
+        fewest = ns[0]
+        for n in ns[1:]:
+            fewest = jnp.minimum(fewest, n)
+        whole = jnp.maximum(lax.div(fewest, CHUNK), 1)
+        tops = lax.fori_loop(1, whole, functools.partial(score, True), tuple(tops))
+        tops = lax.fori_loop(whole, chunks, functools.partial(score, False), tops)
         tops = [jnp.max(m, axis=0, keepdims=True) for m in tops]
 
         for t in TWO:
@@ -227,7 +243,7 @@
                 av[span(c), :] += gv
 
     STEP = 4
-    PARTS = 4
+    PARTS = 8
 
     for part in range(PARTS):
         size = NBLK // PARTS
@@ -282,13 +298,14 @@
             pltpu.VMEM((NSEC, 8, HD), F32),
             pltpu.SMEM((NQ, 32), jnp.int32),
             pltpu.SMEM((NQ,), jnp.int32),
+            pltpu.SMEM((NQ,), jnp.int32),
             pltpu.SMEM((NSEC,), jnp.int32),
             pltpu.SMEM((NSEC,), jnp.int32),
             pltpu.SMEM((NSEC,), jnp.int32),
             pltpu.SMEM(block_section.shape, jnp.int32),
             pltpu.SMEM(section_parent.shape, jnp.int32),
         ] + [pltpu.SMEM(a.shape, jnp.int32) for a in xrefs] + [
-            pltpu.SemaphoreType.DMA((24,)),
+            pltpu.SemaphoreType.DMA((40,)),
         ],
         compiler_params=pltpu.CompilerParams(vmem_limit_bytes=62 * 1024 * 1024),
         cost_estimate=pl.CostEstimate(flops=18_000_000_000, bytes_accessed=24_000_000, transcendentals=12_000_000),
@@ -839,7 +856,7 @@
 def on_device(queries, keys, values, out_weight, d_proj, block_section, section_parent, xref_owner, xref_block, xref_valid):
     seq = lax.axis_size("seq")
     qh, kall, vall, wall, d_attn, *xrefs = gather(
-        queries, keys, values, out_weight.T, d_proj, (xref_owner, xref_block, xref_valid), seq)
+        queries, keys, values, out_weight.T, d_proj, (xref_owner.T, xref_block, xref_valid), seq)
     attn, dq, dk, dv = attention(block_section, section_parent, xrefs, qh, kall, vall, d_attn)
     return hand_on(*scatter(dk, dv, attn, wall, dq, d_proj.shape[1]))
 

time: 188 us -> 185 us (0.984)
  Pallas kernels: 185 us -> 183 us
    pallas_call x1, Pallas kernels: 59.2 us -> 56.5 us  [scatter(): pl.pallas_call(scatter_kernel, out_shape=(jax.ShapeDtypeStruct((T, D), BF...]
where the time goes in v5:
time: 185 us; the launch traced here: 184 us
  Pallas kernels  183 us (99%)
    pallas_call x1, Pallas kernels, gather(): pl.pallas_call(gather_kernel, out_shape=(jax.ShapeDtypeStruct((2 * T, W),...  74.5 us
    pallas_call x1, Pallas kernels, scatter(): pl.pallas_call(scatter_kernel, out_shape=(jax.ShapeDtypeStruct((T, D), BF...  56.5 us
    pallas_call x1, Pallas kernels, attention(): pl.pallas_call(functools.partial(attention_kernel, NBLK, NSEC, NQ, G, XR)...  49.3 us

profile of v5, /device:TPU:1, one launch (start us, length us, event | category | flops | bytes accessed | tf_op | source)
XLA Modules:
  0.0 183.8 jit_solution(8223588949896919078)
XLA Ops:
  0.6 74.5 %shard_map.129 = (bf16[1024,640]{1,0:T(8,128)(2,1)}, bf16[16384,128]{1,0:T(8,128)(2,1)}, bf16[16384,128]{1,0:T(8,128)(2,1)}, bf16[2560,640]{1,0:T(8,128)(2,1)}, ...) custom-call(bf16[512,1280]{1,0:T(8,128)(2,1)} %q_hbm.1, ...), custom_call_target="tpu_custom_call" | custom-call | flops 3400000000 | bytes 40000000 | tf_op jit(solution)/shard_map/pallas_call | solution.py:573
  75.1 49.3 %shard_map.130 = (bf16[1024,640]{1,0:T(8,128)(2,1)}, bf16[1024,640]{1,0:T(8,128)(2,1)}, bf16[16384,128]{1,0:T(8,128)(2,1)}, bf16[16384,128]{1,0:T(8,128)(2,1)}) custom-call(s32[128]{0:T(128)} %sec_hbm.1, s32[16]{0:T(128)} %par_hbm.1, s32[2,1,48]{2,1,0:T(1,128)} %get-tuple-element.20.xo_hbm, s32[2,4,12]{2,1,0:T(4,128)} %get-tuple-element.21.xb_hbm, ...), custom_call_target="tpu_custom_call" | custom-call | flops 17999998976 | bytes 24000000 | tf_op jit(solution)/shard_map/pallas_call | solution.py:275
  124.5 56.5 %shard_map.131 = (bf16[512,640]{1,0:T(8,128)(2,1)}, bf16[512,1280]{1,0:T(8,128)(2,1)}, bf16[512,256]{1,0:T(8,128)(2,1)}, bf16[512,256]{1,0:T(8,128)(2,1)}) custom-call(bf16[16384,128]{1,0:T(8,128)(2,1)} %get-tuple-element.27.dk, bf16[16384,128]{1,0:T(8,128)(2,1)} %get-tuple-element.28.dv, bf16[1024,640]{1,0:T(8,128)(2,1)} %get-tuple-element.29.attn, ...), custom_call_target="tpu_custom_call" | custom-call | flops 3400000000 | bytes 40000000 | tf_op jit(solution)/shard_map/pallas_call | solution.py:789
  181.0 2.6 %shard_map.132 = (bf16[512,640]{1,0:T(8,128)(2,1)}, bf16[512,1280]{1,0:T(8,128)(2,1)}, bf16[512,256]{1,0:T(8,128)(2,1)}, bf16[512,256]{1,0:T(8,128)(2,1)}) custom-call(bf16[512,640]{1,0:T(8,128)(2,1)} %get-tuple-element.32.refs_0_, bf16[512,1280]{1,0:T(8,128)(2,1)} %get-tuple-element.33.refs_1_, bf16[512,256]{1,0:T(8,128)(2,1)} %get-tuple-element.34.refs_2_, ...), custom_call_target="tpu_custom_call" | custom-call | bytes 5000000 | tf_op jit(solution)/shard_map/pallas_call | solution.py:844
